TPU v7x, 512 devices: a whole 4x4x16 slice. The times are simulated.
512 devices in a mesh: dp: 128 (over x, z, core), replica: 4 (over y).
Axes of the slice: x: 4, y: 4, z: 16, core: 2. Of those that a mesh axis runs over, the one named last changes fastest.
Arguments:
- gradient: float32 [8, 512, 27, 512], P(None, 'dp', None, 'replica'), may hold values from -1.2 to 1.2
- block_owner: int32 [216], replicated, may hold values from 0 to 127, as said below
- block_slab: int32 [216], replicated, may hold values from 0 to 7, as said below
- block_col: int32 [216], replicated, may hold values from 0 to 13312, as said below
- left_factor: float32 [384, 512, 512], P('dp', 'replica'), may hold values from -3 to 3
- right_factor: float32 [384, 512, 512], P('dp', 'replica'), may hold values from -3 to 3
- left_root: bfloat16 [384, 512, 512], P('dp', 'replica'), may hold values from -0.25 to 0.25
- right_root: bfloat16 [384, 512, 512], P('dp', None, 'replica'), may hold values from -0.25 to 0.25
Outputs:
- direction: float32 [8, 512, 27, 512], P(None, 'dp', None, 'replica')
- left_new: float32 [384, 512, 512], P('dp', 'replica')
- right_new: float32 [384, 512, 512], P('dp', 'replica')
Inputs may be any that keep to these rules, and one draw needn't show every extreme that they name: `block_owner`: each owner is named by at most 3 entries, and some owner by exactly 3. block_slab and block_col together name every block of the gradient exactly once. `block_col`: a multiple of 512.
All inputs are finite; a program needn't handle non-finite values.
Results may differ from a plain program's by a relative error of at most 0.0003.
Values sent between devices are 32-bit elements; how exact they have to be, the bound alone decides.
No kernel may reach another device: no remote copies, remote signals or barrier semaphores. Data moves between devices by JAX's collectives and lax.ppermute only.
A program may use at most 64 MiB of HBM per device.

v0:
```python
import jax
import jax.numpy as jnp
from jax import lax
from jax.sharding import PartitionSpec as P

BETA = 0.95


def per_device(
    gradient, block_owner, block_slab, block_col, left_factor, right_factor, left_root, right_root
):
    owners = lax.axis_size("dp")
    slot_capacity = left_factor.shape[0]
    quarter = left_factor.shape[1]
    block_side_length = left_factor.shape[2]
    rows_dev = gradient.shape[1]
    block_cols = gradient.shape[2]
    slab_count = gradient.shape[0]
    blocks = block_owner.shape[0]
    position = jnp.arange(blocks, dtype=jnp.int32)
    earlier = position[None, :] < position[:, None]
    same_owner = block_owner[:, None] == block_owner[None, :]
    slot_rank = jnp.sum(jnp.where(earlier & same_owner, 1, 0), axis=1).astype(jnp.int32)
    slot_of_block = block_owner * slot_capacity + slot_rank
    slot_ids = jnp.arange(owners * slot_capacity, dtype=jnp.int32)
    slot_match = slot_of_block[None, :] == slot_ids[:, None]
    slot_live = jnp.any(slot_match, axis=1)
    block_of_slot = jnp.sum(jnp.where(slot_match, position[None, :], 0), axis=1)
    slab_of_slot = block_slab[block_of_slot]
    column_of_slot = block_col[block_of_slot] // block_side_length
    whole_rows = lax.all_gather(gradient, "replica", axis=3, tiled=True)
    selected = whole_rows[slab_of_slot, :, column_of_slot, :]
    selected = jnp.where(slot_live[:, None, None], selected, 0.0)
    complete_block = lax.all_to_all(
        selected.reshape(owners, slot_capacity, rows_dev, whole_rows.shape[3]),
        "dp",
        split_axis=0,
        concat_axis=2,
        tiled=True,
    )[0]
    replica_index = lax.axis_index("replica")
    local_rows = lax.dynamic_slice_in_dim(complete_block, replica_index * quarter, quarter, 1)
    cols_mine = lax.dynamic_slice_in_dim(complete_block, replica_index * quarter, quarter, 2)
    left_statistic_matrix = jnp.einsum(
        "mdz,mxz->mdx", local_rows, complete_block, precision=lax.Precision.HIGHEST
    )
    right_gram = jnp.einsum(
        "caq,cab->cqb", cols_mine, complete_block, precision=lax.Precision.HIGHEST
    )
    left_new = BETA * left_factor + (1.0 - BETA) * left_statistic_matrix
    right_new = BETA * right_factor + (1.0 - BETA) * right_gram
    left_wide = left_root.astype(jnp.float32)
    right_broad_factor = right_root.astype(jnp.float32)
    products = jnp.einsum(
        "cqa,cab->cqb", left_wide, complete_block, precision=lax.Precision.HIGHEST
    )
    directions = jnp.einsum(
        "cra,caq->crq",
        lax.all_gather(products, "replica", axis=1, tiled=True),
        right_broad_factor,
        precision=lax.Precision.HIGHEST,
    )
    outgoing_back = directions.reshape(slot_capacity, owners, rows_dev, quarter)
    returned = lax.all_to_all(outgoing_back, "dp", split_axis=1, concat_axis=0, tiled=True)
    returned = returned.reshape(owners * slot_capacity, rows_dev, quarter)
    tile_of_block = block_slab * block_cols + block_col // block_side_length
    tile_index_list = jnp.arange(blocks, dtype=jnp.int32)
    slot_of_tile = jnp.sum(
        jnp.where(tile_of_block[None, :] == tile_index_list[:, None], slot_of_block[None, :], 0),
        axis=1,
    )
    placed = (
        returned[slot_of_tile]
        .reshape(slab_count, block_cols, rows_dev, quarter)
        .transpose(0, 2, 1, 3)
    )
    return (placed, left_new, right_new)


def solution(mesh):
    return jax.shard_map(
        per_device,
        mesh=mesh,
        in_specs=(
            P(None, "dp", None, "replica"),
            P(),
            P(),
            P(),
            P("dp", "replica", None),
            P("dp", "replica", None),
            P("dp", "replica", None),
            P("dp", None, "replica"),
        ),
        out_specs=(
            P(None, "dp", None, "replica"),
            P("dp", "replica", None),
            P("dp", "replica", None),
        ),
        check_vma=False,
    )
```

profile of v0, /device:TPU:2, one launch (start us, length us, event | category | flops | bytes accessed | tf_op | source)
XLA Modules:
  0.0 352.7 jit_solution(11359161150022987339)
XLA Ops:
  7.2 0.0 copy-start
  7.2 0.0 copy-start.1
  7.2 0.0 all-gather.3.cloned.1.call-start
  7.2 0.7 all-gather.3.cloned.1.call-update
  7.9 0.0 all-gather.5.cloned.1.call-start
  8.0 0.9 select_reduce_fusion.2
  8.9 0.7 fusion.13
  9.6 0.1 select_reduce_fusion
  9.8 3.6 %gather_fusion = s32[384]{0:T(512)S(1)} fusion(s32[216]{0:T(256)} %param.10, s32[1024]{0:T(1024)S(1)} %pad_clamp_fusion.1), kind=kCustom, calls=%fused_computation | custom fusion | bytes 4608 | tf_op jit(solution)/shard_map/gather | solution.py:29
  13.4 0.0 copy-done.1
  13.4 2.8 gather_fusion.1
  16.2 0.1 fusion.4
  16.4 0.8 broadcast_in_dim.62
  17.2 36.9 %all-gather.3.cloned.1.call-done = f32[8,4,27,512]{3,1,2,0:T(4,128)} async-done(((f32[8,4,27,128]{3,1,2,0:T(4,128)}), f32[8,4,27,512]{3,1,2,0:T(4,128)}) %all-gather.3.cloned.1.call-update) | async-done | bytes 1769488 | tf_op jit(solution)/shard_map/all_gather | solution.py:31
  54.1 6.3 %gather_fusion.2 = f32[384,4,512]{2,1,0:T(4,128)S(1)} fusion(f32[8,4,27,512]{3,1,2,0:T(4,128)} %all-gather.3.cloned.1.call-done, s32[384]{0:T(512)S(1)} %fusion.12), kind=kCustom, calls=%fused_computation.2 | custom fusion | bytes 6294528 | tf_op jit(solution)/shard_map/gather | solution.py:32
  60.4 1.6 broadcast_select_fusion
  62.1 160.0 %all_to_all.30 = f32[128,3,4,512]{3,2,1,0:T(4,128)S(1)} all-to-all(f32[128,3,4,512]{3,2,1,0:T(4,128)S(1)} %broadcast_select_fusion), channel_id=1, replica_groups=mesh['dp'=128,'replica'=4] {'dp'}, dimensions={0} | all-to-all | bytes 6291456 | tf_op jit(solution)/shard_map/all_to_all | solution.py:34
  222.1 2.3 copy.28
  224.4 3.2 squeeze.3
  227.6 0.0 copy-done
  227.6 3.5 %convolution_bitcast_fusion = f32[3,128,512]{1,2,0:T(8,128)} fusion(f32[3,512,512]{2,1,0:T(8,128)S(1)} %squeeze.3, bf16[3,128,512]{2,1,0:T(8,128)(2,1)S(1)} %copy-done), kind=kOutput, calls=%fused_computation.5 | convolution fusion | flops 1207959552 | bytes 4325376 | tf_op jit(solution)/shard_map/cqa,cab->cqb/dot_general | solution.py:54
  231.2 0.0 all-gather.5.cloned.1.call-update
  231.2 44.7 %all-gather.5.cloned.1.call-done = f32[3,512,512]{1,2,0:T(8,128)} async-done(((f32[3,128,512]{1,2,0:T(8,128)}), f32[3,512,512]{1,2,0:T(8,128)}) %all-gather.5.cloned.1.call-update) | async-done | bytes 3145744 | tf_op jit(solution)/shard_map/all_gather | solution.py:59
  275.8 4.6 %fusion.16 = f32[3,512,128]{2,1,0:T(8,128)S(1)} fusion(f32[3,512,512]{1,2,0:T(8,128)} %all-gather.5.cloned.1.call-done, bf16[3,512,128]{2,1,0:T(8,128)(2,1)} %param.15), kind=kOutput, calls=%fused_computation.45 | convolution fusion | flops 1207959552 | bytes 4325376 | tf_op jit(solution)/shard_map/cra,caq->crq/dot_general | solution.py:57
  280.5 1.0 copy.31
  281.5 17.0 %all-to-all-start.1 = ((f32[3,128,4,128]{3,2,0,1:T(4,128)}), f32[3,128,4,128]{3,2,0,1:T(4,128)}, u32[]{:S(2)}, u32[]{:S(2)}) async-start(f32[3,128,4,128]{3,2,0,1:T(4,128)} %copy.31), calls=%async_computation.1 | async-start | bytes 1572864 | tf_op jit(solution)/shard_map/all_to_all | solution.py:64
  298.5 0.0 copy-start.2
  298.5 0.1 select_reduce_fusion.1
  298.7 4.1 %fusion = f32[3,128,512]{2,1,0:T(8,128)} fusion(f32[3,512,512]{2,1,0:T(8,128)S(1)} %squeeze.3, s32[]{:T(128)S(6)} %select_n.89, f32[3,128,512]{2,1,0:T(8,128)} %param.13), kind=kOutput, calls=%fused_computation.7 | convolution fusion | flops 1208549376 | bytes 5505028 | tf_op jit(solution)/shard_map/caq,cab->cqb/dot_general | solution.py:47
  302.8 0.0 copy-done.2
  302.8 4.2 %fusion.1 = f32[3,128,512]{2,1,0:T(8,128)} fusion(f32[3,512,512]{2,1,0:T(8,128)S(1)} %squeeze.3, s32[]{:T(128)S(6)} %select_n.89, f32[3,128,512]{2,1,0:T(8,128)S(1)} %copy-done.2), kind=kOutput, calls=%fused_computation.9 | convolution fusion | flops 1208549376 | bytes 5505028 | tf_op jit(solution)/shard_map/mdz,mxz->mdx/dot_general | solution.py:44
  307.0 36.0 %all-to-all-done.1 = f32[3,128,4,128]{3,2,0,1:T(4,128)} async-done(((f32[3,128,4,128]{3,2,0,1:T(4,128)}), f32[3,128,4,128]{3,2,0,1:T(4,128)}, u32[]{:S(2)}, u32[]{:S(2)}) %all-to-all-start.1) | async-done | bytes 786464 | tf_op jit(solution)/shard_map/all_to_all | solution.py:64
  343.1 2.8 gather_fusion.3
  (5 shorter events, 0.1 us)
Async XLA Ops:
  7.2 220.5 %copy-start = (bf16[3,128,512]{2,1,0:T(8,128)(2,1)S(1)}, bf16[3,128,512]{2,1,0:T(8,128)(2,1)}, u32[]{:S(2)}) copy-start(bf16[3,128,512]{2,1,0:T(8,128)(2,1)} %param.14) | copy-start | bytes 1179652
  7.2 6.2 %copy-start.1 = (s32[216]{0:T(256)S(1)}, s32[216]{0:T(256)}, u32[]{:S(2)}) copy-start(s32[216]{0:T(256)} %param.11) | copy-start | bytes 2596
  7.2 46.9 %all-gather.3.cloned.1.call-start = ((), (), s32[]{:S(2)}) async-start(), calls=%async_computation.2 | async-start | bytes 2211840 | tf_op jit(solution)/shard_map/all_gather | solution.py:31
  7.9 267.9 %all-gather.5.cloned.1.call-start = ((), (), s32[]{:S(2)}) async-start(), calls=%async_computation.3 | async-start | bytes 3932160 | tf_op jit(solution)/shard_map/all_gather | solution.py:59
  281.5 61.5 %all-to-all-start.1 = ((f32[3,128,4,128]{3,2,0,1:T(4,128)}), f32[3,128,4,128]{3,2,0,1:T(4,128)}, u32[]{:S(2)}, u32[]{:S(2)}) async-start(f32[3,128,4,128]{3,2,0,1:T(4,128)} %copy.31), calls=%async_computation.1 | async-start | bytes 1572864 | tf_op jit(solution)/shard_map/all_to_all | solution.py:64
  298.5 4.3 %copy-start.2 = (f32[3,128,512]{2,1,0:T(8,128)S(1)}, f32[3,128,512]{2,1,0:T(8,128)}, u32[]{:S(2)}) copy-start(f32[3,128,512]{2,1,0:T(8,128)} %param.12) | copy-start | bytes 2359300
Sparse Core Ops, SparseCore 0:
  10.1 43.9 all-gather.2
  231.3 44.4 all-gather.4
where the time goes:
time: 353 us
  blocking collectives  160 us (45%)
  waiting for transfers between devices  118 us (33%)
  local copies, waits for them, and re-layouts  23 us (7%)
  starting transfers between devices  17.1 us (5%)
  matrix products  16.5 us (5%)
  between operations  14.2 us (4%)
  other arithmetic  3.72 us (1%)
    all_to_all x1, blocking collectives, per_device(): lax.all_to_all(selected.reshape(owners, slot_capacity, rows_dev, whole_ro...  160 us
    all_gather x1, waiting for transfers between devices, per_device(): lax.all_gather(products, 'replica', axis=1, tiled=True)  44.7 us
    all_gather x1, waiting for transfers between devices, per_device(): whole_rows = lax.all_gather(gradient, 'replica', axis=3, tiled=True)  36.9 us
    all_to_all x1, waiting for transfers between devices, per_device(): lax.all_to_all(outgoing_back, 'dp', split_axis=1, concat_axis=0, tiled=True)  36 us
    all_to_all x1, starting transfers between devices, per_device(): lax.all_to_all(outgoing_back, 'dp', split_axis=1, concat_axis=0, tiled=True)  17 us
  transfers between devices with their start and end apart: 3, of which 3 were waited for; matrix products, arithmetic and copies ran while one was open for 5% of the time, Pallas kernels for 0%

commit v1 on v0

v1 whole, which is shorter than its diff:
```python
import functools

import jax
import jax.numpy as jnp
from jax import lax
from jax.experimental import pallas as pl
from jax.experimental.pallas import tpu as pltpu
from jax.sharding import Mesh
from jax.sharding import PartitionSpec as P

BETA = 0.95
STRIDE = 32
VMEM_BYTES = 24 * 1024 * 1024
F32 = jnp.float32
BF16 = jnp.bfloat16
SMEM_SPEC = pl.BlockSpec(memory_space=pltpu.SMEM)
VMEM_SPEC = pl.BlockSpec(memory_space=pltpu.VMEM)


def call(body, name, out_shape, out_specs, in_specs, scratch=(), flops=0, moved=1_000_000, vmem=VMEM_BYTES):
    return pl.pallas_call(
        body,
        out_shape=out_shape,
        in_specs=in_specs,
        out_specs=out_specs,
        scratch_shapes=list(scratch),
        compiler_params=pltpu.CompilerParams(vmem_limit_bytes=vmem),
        cost_estimate=pl.CostEstimate(flops=flops, bytes_accessed=moved, transcendentals=0),
        name=name,
    )


def log2(size):
    return size.bit_length() - 1


def capacities(plane_slots):
    return sorted({plane_slots * 3 // 4, plane_slots * 5 // 6, plane_slots})


def select_kernel(sizes, owner_hbm, slab_hbm, col_hbm, grad_hbm, *refs):
    blocks, owners, cap, x_size, z_size, core_size, y_size, cols, side = sizes
    tiers = capacities(x_size * core_size * cap)
    send_refs, refs = refs[: len(tiers)], refs[len(tiers) :]
    plan_ref, tier_ref, owner_ref, slab_ref, col_ref, grad_ref, pack_ref = refs[:7]
    count_ref, fill_ref, sems = refs[7:]
    stride = pack_ref.shape[1]
    copies = [
        pltpu.make_async_copy(source, target, sems.at[i])
        for i, (source, target) in enumerate(
            ((owner_hbm, owner_ref), (slab_hbm, slab_ref), (col_hbm, col_ref), (grad_hbm, grad_ref))
        )
    ]
    for copy in copies:
        copy.start()

    def clear(o, carry):
        count_ref[o] = 0
        return carry

    lax.fori_loop(0, owners, clear, 0, unroll=16)
    for z in range(z_size):
        fill_ref[z] = 0
    for s in range(stride):
        plan_ref[blocks + s] = y_size - 1
    plan_ref[blocks + 2 * stride] = lax.axis_index("y")
    z_here = lax.axis_index("z")
    for copy in copies:
        copy.wait()

    def move(k, carry):
        o = owner_ref[k]
        rank = count_ref[o]
        count_ref[o] = rank + 1
        core = o & (core_size - 1)
        z = (o >> log2(core_size)) & (z_size - 1)
        x = o >> (log2(core_size) + log2(z_size))
        spot = fill_ref[z]
        fill_ref[z] = spot + 1
        tile = slab_ref[k] * cols + (col_ref[k] >> log2(side))
        plan_ref[tile] = z * stride + spot
        slot = (x * core_size + core) * y_size + rank
        plan_ref[spot + jnp.where(z == z_here, blocks, blocks + stride)] = slot
        pack_ref[z, spot] = grad_ref[tile]
        return carry

    lax.fori_loop(0, blocks, move, 0, unroll=24)
    most = fill_ref[0]
    for z in range(1, z_size):
        most = jnp.maximum(most, fill_ref[z])
    tier = jnp.int32(len(tiers) - 1)
    for i in range(len(tiers) - 2, -1, -1):
        tier = jnp.where(most <= tiers[i], i, tier)
    tier_ref[0] = tier
    for i, send_ref in enumerate(send_refs):

        @pl.when(tier == i)
        def _():
            copy = pltpu.make_async_copy(pack_ref.at[:, : tiers[i]], send_ref, sems.at[4])
            copy.start()
            copy.wait()


def place_kernel(plan_ref, back_ref, out_ref):
    bits = log2(STRIDE)

    def step(t, carry):
        code = plan_ref[t]
        out_ref[t] = back_ref[code >> bits, code & (STRIDE - 1)]
        return carry

    lax.fori_loop(0, out_ref.shape[0], step, 0, unroll=8)


def forward_kernel(cap, blocks, plan_ref, in_ref, *refs):
    out_ref = refs[-1]
    planes, y_size = out_ref.shape[:2]
    for p in range(planes):
        out_ref[p, :cap] = jnp.zeros_like(out_ref[p, :cap])
    for spot in range(in_ref.shape[1]):
        slot = plan_ref[blocks + spot]
        out_ref[slot >> log2(y_size), slot & (y_size - 1)] = in_ref[:, spot]


def backward_kernel(blocks, plan_ref, in_ref, after_ref, out_ref):
    y_size = in_ref.shape[1]
    for spot in range(out_ref.shape[1]):
        slot = plan_ref[blocks + spot]
        out_ref[:, spot] = in_ref[slot >> log2(y_size), slot & (y_size - 1)]


def around(position, size):
    return position & (size - 1)


def roots_kernel(plan_ref, left_ref, right_ref, *out_refs):
    parts = len(out_refs)
    quarter = left_ref.shape[1]
    for d, out_ref in enumerate(out_refs):
        s = jnp.minimum(around(plan_ref[plan_ref.shape[0] - 1] + d, parts), left_ref.shape[0] - 1)
        left = left_ref[s].astype(F32)
        right = right_ref[s].astype(F32)
        for j in range(parts):
            out_ref[j] = left[:, j * quarter : (j + 1) * quarter]
            out_ref[parts + j] = right[j * quarter : (j + 1) * quarter]


def split(value):
    high = value.astype(BF16)
    return high, (value - high.astype(F32)).astype(BF16)


def dot(a, b, a_dim, b_dim):
    return lax.dot_general(a, b, (((a_dim,), (b_dim,)), ((), ())), preferred_element_type=F32)


def direction_kernel(plan_ref, in_ref, *refs):
    x_size, core_size, parts, z_size, rows, width = in_ref.shape
    pieces, (out_ref, block_ref, left_ref, right_ref, result_ref) = refs[:parts], refs[parts:]
    side = parts * width
    for x in range(x_size):
        for c in range(core_size):
            for q in range(parts):
                block_ref[
                    x * z_size : (x + 1) * z_size, c * rows : (c + 1) * rows, q * width : (q + 1) * width
                ] = in_ref[x, c, q]
    for d, piece in enumerate(pieces):
        q = around(plan_ref[plan_ref.shape[0] - 1] - d, parts)
        for j in range(parts):
            left_ref[pl.ds(q * width, width), j * width : (j + 1) * width] = piece[j].astype(BF16)
            right_ref[q, j * width : (j + 1) * width, :] = piece[parts + j].astype(BF16)
    high, low = split(block_ref[...].reshape(side, side))
    right = jnp.concatenate([right_ref[q] for q in range(parts)], axis=1)
    product = dot(high, right, 1, 0) + dot(low, right, 1, 0)
    high, low = split(product)
    left = left_ref[...]
    result_ref[...] = (dot(left, high, 1, 0) + dot(left, low, 1, 0)).reshape(result_ref.shape)
    for x in range(x_size):
        for c in range(core_size):
            for q in range(parts):
                out_ref[x, c, q] = result_ref[
                    x * z_size : (x + 1) * z_size, c * rows : (c + 1) * rows, q * width : (q + 1) * width
                ]


def grams_kernel(plan_ref, block_ref, *refs):
    out_refs, gram_ref = refs[:-1], refs[-1]
    parts = len(out_refs)
    quarter = out_refs[0].shape[1]
    side = block_ref.shape[2]
    high, low = split(block_ref[...].reshape(side, side))
    for i, dim in enumerate((1, 0)):
        gram_ref[i] = dot(high, high, dim, dim) + (dot(high, low, dim, dim) + dot(low, high, dim, dim))
    for d, out_ref in enumerate(out_refs):
        q = around(plan_ref[plan_ref.shape[0] - 1] + d, parts)
        out_ref[...] = gram_ref[:, pl.ds(q * quarter, quarter), :]


def factors_kernel(plan_ref, after_ref, left_ref, right_ref, *refs):
    pieces, (left_out, right_out) = refs[:-2], refs[-2:]
    for d, piece in enumerate(pieces):
        s = around(plan_ref[plan_ref.shape[0] - 1] - d, len(pieces))

        @pl.when(s < left_ref.shape[0])
        def _():
            left_out[s] = BETA * left_ref[s] + (1.0 - BETA) * piece[0]
            right_out[s] = BETA * right_ref[s] + (1.0 - BETA) * piece[1]


def exchange(value, axes):
    return lax.all_to_all(value, axes, split_axis=0, concat_axis=0, tiled=True)


def spread(pieces):
    size = len(pieces)
    turn = lambda d: [(i, (i + d) % size) for i in range(size)]
    return [pieces[0]] + [lax.ppermute(pieces[d], "y", turn(d)) for d in range(1, size)]


def shape(*dims):
    return jax.ShapeDtypeStruct(dims, F32)


def step(index, blocks, plan, sends, left_factor, right_factor, left_root, right_root):
    x_size, z_size = lax.axis_size("x"), lax.axis_size("z")
    core_size, y_size = lax.axis_size("core"), lax.axis_size("y")
    planes = x_size * core_size
    cap, quarter, side = left_factor.shape
    send = sends[index]
    _, capacity, rows, width = send.shape
    cube = side * side * side * 2

    roots = spread(
        call(
            roots_kernel,
            "roots",
            (shape(2 * y_size, quarter, quarter),) * y_size,
            (VMEM_SPEC,) * y_size,
            [SMEM_SPEC, VMEM_SPEC, VMEM_SPEC],
        )(plan, left_root, right_root)
    )

    moved = exchange(send, "z")
    moved = call(
        functools.partial(forward_kernel, cap, blocks),
        "forward",
        shape(planes, y_size, z_size, rows, width),
        VMEM_SPEC,
        [SMEM_SPEC, VMEM_SPEC] + [pl.BlockSpec(memory_space=pl.ANY)] * y_size,
    )(plan, moved, *roots)
    moved = exchange(moved.reshape(planes * y_size, z_size, rows, width), ("x", "core", "y"))

    directions, block = call(
        direction_kernel,
        "direction",
        (
            shape(x_size, core_size, y_size, z_size, rows, width),
            pltpu.HBM((x_size * z_size, core_size * rows, side), F32),
        ),
        (VMEM_SPEC, VMEM_SPEC),
        [SMEM_SPEC, VMEM_SPEC] + [VMEM_SPEC] * y_size,
        [
            pltpu.VMEM((side, side), BF16),
            pltpu.VMEM((y_size, side, width), BF16),
            pltpu.VMEM((x_size * z_size, core_size * rows, side), F32),
        ],
        flops=4 * cube,
        moved=6_000_000,
    )(plan, moved.reshape(x_size, core_size, y_size, z_size, rows, width), *roots)

    grams = spread(
        call(
            grams_kernel,
            "grams",
            (shape(2, quarter, side),) * y_size,
            (VMEM_SPEC,) * y_size,
            [SMEM_SPEC, VMEM_SPEC],
            [pltpu.VMEM((2, side, side), F32)],
            flops=6 * cube,
            moved=5_000_000,
        )(plan, block)
    )
    back = exchange(directions.reshape(planes * y_size, z_size, rows, width), ("x", "core", "y"))
    back = call(
        functools.partial(backward_kernel, blocks),
        "backward",
        shape(z_size, capacity, rows, width),
        VMEM_SPEC,
        [SMEM_SPEC, VMEM_SPEC, pl.BlockSpec(memory_space=pl.ANY)],
    )(plan, back.reshape(planes, y_size, z_size, rows, width), grams[0])
    back = exchange(back, "z")

    result = pltpu.HBM((blocks, rows, width), F32)
    placed = call(place_kernel, "place", result, VMEM_SPEC, [SMEM_SPEC, VMEM_SPEC])(
        plan, back
    )
    left_new, right_new = call(
        factors_kernel,
        "factors",
        (shape(*left_factor.shape), shape(*right_factor.shape)),
        (VMEM_SPEC, VMEM_SPEC),
        [SMEM_SPEC, pl.BlockSpec(memory_space=pl.ANY)] + [VMEM_SPEC] * (2 + y_size),
        moved=5_000_000,
    )(plan, placed, left_factor, right_factor, *grams)

    return placed, left_new, right_new


def per_device(
    gradient, block_owner, block_slab, block_col, left_factor, right_factor, left_root, right_root
):
    x_size, z_size = lax.axis_size("x"), lax.axis_size("z")
    core_size, y_size = lax.axis_size("core"), lax.axis_size("y")
    owners = x_size * z_size * core_size
    cap, quarter, side = left_factor.shape
    slabs, rows, cols, width = gradient.shape
    blocks = block_owner.shape[0]
    tiers = capacities(x_size * core_size * cap)
    assert tiers[-1] <= STRIDE and cap < y_size
    index = lambda size: jax.ShapeDtypeStruct((size,), jnp.int32)
    any_spec = pl.BlockSpec(memory_space=pl.ANY)

    sizes = (blocks, owners, cap, x_size, z_size, core_size, y_size, cols, side)
    *sends, plan, tier = call(
        functools.partial(select_kernel, sizes),
        "select",
        tuple(shape(z_size, capacity, rows, width) for capacity in tiers)
        + (index(blocks + 2 * STRIDE + 1), index(1)),
        (any_spec,) * len(tiers) + (SMEM_SPEC,) * 2,
        [any_spec] * 4,
        [pltpu.SMEM((blocks,), jnp.int32)] * 3
        + [pltpu.VMEM((blocks, rows, width), F32), pltpu.VMEM((z_size, STRIDE, rows, width), F32)]
        + [pltpu.SMEM((owners,), jnp.int32), pltpu.SMEM((z_size,), jnp.int32), pltpu.SemaphoreType.DMA((5,))],
        moved=3_000_000,
        vmem=63 * 1024 * 1024,
    )(
        block_owner,
        block_slab,
        block_col,
        gradient.transpose(0, 2, 1, 3).reshape(blocks, rows, width),
    )
    placed, left_new, right_new = lax.switch(
        tier[0],
        [functools.partial(step, i, blocks) for i in range(len(tiers))],
        plan,
        sends,
        left_factor,
        right_factor,
        left_root,
        right_root,
    )
    placed = placed.reshape(slabs, cols, rows, width).transpose(0, 2, 1, 3)
    return placed, left_new, right_new


def solution(mesh, sizes=(4, 16, 2, 4)):
    fine = Mesh(mesh.devices.reshape(sizes), ("x", "z", "core", "y"))
    dp = ("x", "z", "core")
    return jax.shard_map(
        per_device,
        mesh=fine,
        in_specs=(
            P(None, dp, None, "y"),
            P(),
            P(),
            P(),
            P(dp, "y", None),
            P(dp, "y", None),
            P(dp, "y", None),
            P(dp, None, "y"),
        ),
        out_specs=(P(None, dp, None, "y"), P(dp, "y", None), P(dp, "y", None)),
        check_vma=False,
    )
```

time: 353 us -> 152 us (0.43)
  the two profiles are of different devices: /device:TPU:2 before, /device:TPU:32 now
where the time goes in v1:
time: 152 us; the launch traced here: 151 us
  waiting for transfers between devices  53.7 us (35%)
  starting transfers between devices  52.2 us (34%)
  blocking collectives  24.2 us (16%)
  Pallas kernels  19.3 us (13%)
    all_to_all x3, waiting for transfers between devices, exchange(): return lax.all_to_all(value, axes, split_axis=0, concat_axis=0, tiled=True)  35.3 us
    all_to_all x3, starting transfers between devices, exchange(): return lax.all_to_all(value, axes, split_axis=0, concat_axis=0, tiled=True)  30.8 us
    all_to_all x1, blocking collectives, exchange(): return lax.all_to_all(value, axes, split_axis=0, concat_axis=0, tiled=True)  24.2 us
    ppermute x6, starting transfers between devices, spread(): lax.ppermute(pieces[d], 'y', turn(d))  21.4 us
    ppermute x6, waiting for transfers between devices, spread(): lax.ppermute(pieces[d], 'y', turn(d))  18.5 us
    pallas_call x1, Pallas kernels, per_device(): call(functools.partial(select_kernel, sizes), 'select', tuple((shape(z_si...  5.04 us
    pallas_call x1, Pallas kernels, step(): call(grams_kernel, 'grams', (shape(2, quarter, side),) * y_size, (VMEM_SP...  3.54 us
    pallas_call x1, Pallas kernels, step(): call(direction_kernel, 'direction', (shape(x_size, core_size, y_size, z_s...  3.29 us
  transfers between devices with their start and end apart: 9, of which 6 were waited for; matrix products, arithmetic and copies ran while one was open for 0% of the time, Pallas kernels for 4%

profile of v1, /device:TPU:32, one launch (start us, length us, event | category | flops | bytes accessed | tf_op | source)
XLA Modules:
  0.0 150.9 jit_solution(10178957408185555750)
XLA Ops:
  0.6 0.0 copy-start.6
  0.6 5.0 %select.1 = (f32[16,18,4,128]{3,2,1,0:T(4,128)}, f32[16,20,4,128]{3,2,1,0:T(4,128)}, f32[16,24,4,128]{3,2,1,0:T(4,128)}, s32[281]{0:T(512)S(1)}, s32[1]{0:T(128)}) custom-call(s32[216]{0:T(256)} %owner_hbm.1, s32[216]{0:T(256)} %slab_hbm.1, s32[216]{0:T(256)} %col_hbm.1, f32[216,4,128]{2,1,0:T(4,128)} %bitcast.29), custom_call_target="tpu_custom_call" | custom-call | bytes 3000000 | tf_op jit(solution)/shard_map/select/pallas_call | solution.py:324
  6.3 0.0 copy-done.6
  6.4 144.6 %conditional.1 = (f32[216,4,128]{2,1,0:T(4,128)}, f32[3,128,512]{2,1,0:T(8,128)}, f32[3,128,512]{2,1,0:T(8,128)}) conditional(s32[]{:T(128)} %bitcast.14, (f32[16,18,4,128]{3,2,1,0:T(4,128)}, s32[281]{0:T(512)S(1)}, bf16[3,128,512]{2,1,0:T(8,128)(2,1)S(1)}, bf16[3,512,128]{2,1,0:T(8,128)(2,1)}, f32[3,128,512]{2,1,0:T(8,128)}, ...), branch_computations={%region_0.0_spmd, %region_1.0_spmd, %region_2.0_spmd} | conditional | flops 2684354560 | bytes 51457724 | solution.py:342
  6.4 0.0 copy-start.7
  6.4 15.4 %all-to-all-start = ((f32[16,18,4,128]{3,2,1,0:T(4,128)}), f32[16,18,4,128]{3,2,1,0:T(4,128)S(1)}, u32[]{:S(2)}, u32[]{:S(2)}) async-start(f32[16,18,4,128]{3,2,1,0:T(4,128)} %get-tuple-element.37), calls=%async_computation | async-start | bytes 1179648 | tf_op jit(solution)/shard_map/cond/branch_0_fun/all_to_all | solution.py:211
  21.7 0.0 copy-done.7
  21.7 0.7 roots.3
  22.4 3.5 %collective-permute-start = (f32[8,128,128]{2,1,0:T(8,128)S(1)}, f32[8,128,128]{2,1,0:T(8,128)S(1)}, u32[]{:S(2)}, u32[]{:S(2)}) collective-permute-start(f32[8,128,128]{2,1,0:T(8,128)S(1)} %get-tuple-element.41), channel_id=1, source_target_pairs={{0,1},{1,2},{2,3},{3,0},{4,5},{5,6},{6,7},{7,4},{8,9},{9,10},{10,1... | collective-permute-start | bytes 1572872 | tf_op jit(solution)/shard_map/cond/branch_0_fun/ppermute | solution.py:217
  25.9 4.8 %collective-permute-start.1 = (f32[8,128,128]{2,1,0:T(8,128)S(1)}, f32[8,128,128]{2,1,0:T(8,128)S(1)}, u32[]{:S(2)}, u32[]{:S(2)}) collective-permute-start(f32[8,128,128]{2,1,0:T(8,128)S(1)} %get-tuple-element.42), channel_id=1, source_target_pairs={{0,2},{1,3},{2,0},{3,1},{4,6},{5,7},{6,4},{7,5},{8,10},{9,11},{10,... | collective-permute-start | bytes 1572872 | tf_op jit(solution)/shard_map/cond/branch_0_fun/ppermute | solution.py:217
  30.8 3.3 %collective-permute-start.2 = (f32[8,128,128]{2,1,0:T(8,128)S(1)}, f32[8,128,128]{2,1,0:T(8,128)S(1)}, u32[]{:S(2)}, u32[]{:S(2)}) collective-permute-start(f32[8,128,128]{2,1,0:T(8,128)S(1)} %get-tuple-element.43), channel_id=1, source_target_pairs={{0,3},{1,0},{2,1},{3,2},{4,7},{5,4},{6,5},{7,6},{8,11},{9,8},{10,9... | collective-permute-start | bytes 1572872 | tf_op jit(solution)/shard_map/cond/branch_0_fun/ppermute | solution.py:217
  34.0 5.3 %collective-permute-done.refs_1_ = f32[8,128,128]{2,1,0:T(8,128)S(1)} collective-permute-done((f32[8,128,128]{2,1,0:T(8,128)S(1)}, f32[8,128,128]{2,1,0:T(8,128)S(1)}, u32[]{:S(2)}, u32[]{:S(2)}) %collective-permute-start) | collective-permute-done | bytes 524320 | tf_op jit(solution)/shard_map/cond/branch_0_fun/ppermute | solution.py:217
  39.3 11.8 %collective-permute-done.1.refs_2_ = f32[8,128,128]{2,1,0:T(8,128)S(1)} collective-permute-done((f32[8,128,128]{2,1,0:T(8,128)S(1)}, f32[8,128,128]{2,1,0:T(8,128)S(1)}, u32[]{:S(2)}, u32[]{:S(2)}) %collective-permute-start.1) | collective-permute-done | bytes 524320 | tf_op jit(solution)/shard_map/cond/branch_0_fun/ppermute | solution.py:217
  51.1 1.4 collective-permute-done.2.refs_3_
  52.5 0.6 all-to-all-done.in_ref
  53.1 0.8 forward.3
  53.9 24.2 %all_to_all.48 = f32[32,16,4,128]{3,2,1,0:T(4,128)S(1)} all-to-all(f32[32,16,4,128]{3,2,1,0:T(4,128)S(1)} %bitcast.19), channel_id=1, replica_groups=mesh['x'=4,'z'=16,'core'=2,'y'=4] {'x','core','y'}, dimensions={0} | all-to-all | bytes 2097152 | tf_op jit(solution)/shard_map/cond/branch_0_fun/all_to_all | solution.py:211
  78.1 3.3 %direction.3 = (f32[4,2,4,16,4,128]{5,4,3,2,1,0:T(4,128)}, f32[64,8,512]{2,1,0:T(8,128)}) custom-call(s32[281]{0:T(512)S(1)} %get-tuple-element.36.plan_ref, f32[4,2,4,16,4,128]{5,4,3,2,1,0:T(4,128)S(1)} %bitcast.25, f32[8,128,128]{2,1,0:T(8,128)S(1)} %get-tuple-element.40.refs_0_, f32[8,128,128]{2,1,0:T(8,128)S(1)} %collective-permute-done.refs_1_, ...), custom_call_target="tpu_custom_call" | custom-call | flops 1073741824 | bytes 6000000 | tf_op jit(solution)/shard_map/cond/branch_0_fun/direction/pallas_call | solution.py:253
  81.4 0.0 copy-start
  81.4 4.1 %all-to-all-start.2 = ((f32[32,16,4,128]{3,2,1,0:T(4,128)}), f32[32,16,4,128]{3,2,1,0:T(4,128)S(1)}, u32[]{:S(2)}, u32[]{:S(2)}) async-start(f32[32,16,4,128]{3,2,1,0:T(4,128)} %bitcast.2), calls=%async_computation.2 | async-start | bytes 2097152 | tf_op jit(solution)/shard_map/cond/branch_0_fun/all_to_all | solution.py:211
  85.5 0.0 copy-done
  85.5 3.5 %grams.3 = (f32[2,128,512]{2,1,0:T(8,128)S(1)}, f32[2,128,512]{2,1,0:T(8,128)}, f32[2,128,512]{2,1,0:T(8,128)}, f32[2,128,512]{2,1,0:T(8,128)S(1)}) custom-call(s32[281]{0:T(512)S(1)} %get-tuple-element.36.plan_ref, f32[64,8,512]{2,1,0:T(8,128)S(1)} %copy-done), custom_call_target="tpu_custom_call" | custom-call | flops 1610612736 | bytes 5000000 | tf_op jit(solution)/shard_map/cond/branch_0_fun/grams/pallas_call | solution.py:272
  89.0 13.6 %all-to-all-done.2 = f32[32,16,4,128]{3,2,1,0:T(4,128)S(1)} async-done(((f32[32,16,4,128]{3,2,1,0:T(4,128)}), f32[32,16,4,128]{3,2,1,0:T(4,128)S(1)}, u32[]{:S(2)}, u32[]{:S(2)}) %all-to-all-start.2) | async-done | bytes 1048608 | tf_op jit(solution)/shard_map/cond/branch_0_fun/all_to_all | solution.py:211
  102.6 1.5 backward.3
  104.1 11.3 %all-to-all-start.3 = ((f32[16,18,4,128]{3,2,1,0:T(4,128)}), f32[16,18,4,128]{3,2,1,0:T(4,128)S(1)}, u32[]{:S(2)}, u32[]{:S(2)}) async-start(f32[16,18,4,128]{3,2,1,0:T(4,128)} %backward.3), calls=%async_computation.3 | async-start | bytes 1179648 | tf_op jit(solution)/shard_map/cond/branch_0_fun/all_to_all | solution.py:211
  115.4 1.9 %collective-permute-start.3 = (f32[2,128,512]{2,1,0:T(8,128)}, f32[2,128,512]{2,1,0:T(8,128)S(1)}, u32[]{:S(2)}, u32[]{:S(2)}) collective-permute-start(f32[2,128,512]{2,1,0:T(8,128)} %get-tuple-element.49), channel_id=1, source_target_pairs={{0,1},{1,2},{2,3},{3,0},{4,5},{5,6},{6,7},{7,4},{8,9},{9,10},{10,1... | collective-permute-start | bytes 1572872 | tf_op jit(solution)/shard_map/cond/branch_0_fun/ppermute | solution.py:217
  117.4 4.6 %collective-permute-start.4 = (f32[2,128,512]{2,1,0:T(8,128)}, f32[2,128,512]{2,1,0:T(8,128)S(1)}, u32[]{:S(2)}, u32[]{:S(2)}) collective-permute-start(f32[2,128,512]{2,1,0:T(8,128)} %get-tuple-element.50), channel_id=1, source_target_pairs={{0,2},{1,3},{2,0},{3,1},{4,6},{5,7},{6,4},{7,5},{8,10},{9,11},{10,... | collective-permute-start | bytes 1572872 | tf_op jit(solution)/shard_map/cond/branch_0_fun/ppermute | solution.py:217
  122.0 3.3 %collective-permute-start.5 = (f32[2,128,512]{2,1,0:T(8,128)S(1)}, f32[2,128,512]{2,1,0:T(8,128)S(1)}, u32[]{:S(2)}, u32[]{:S(2)}) collective-permute-start(f32[2,128,512]{2,1,0:T(8,128)S(1)} %get-tuple-element.51), channel_id=1, source_target_pairs={{0,3},{1,0},{2,1},{3,2},{4,7},{5,4},{6,5},{7,6},{8,11},{9,8},{10,9... | collective-permute-start | bytes 1572872 | tf_op jit(solution)/shard_map/cond/branch_0_fun/ppermute | solution.py:217
  125.3 21.1 %all-to-all-done.3.back_ref = f32[16,18,4,128]{3,2,1,0:T(4,128)S(1)} async-done(((f32[16,18,4,128]{3,2,1,0:T(4,128)}), f32[16,18,4,128]{3,2,1,0:T(4,128)S(1)}, u32[]{:S(2)}, u32[]{:S(2)}) %all-to-all-start.3) | async-done | bytes 589856 | tf_op jit(solution)/shard_map/cond/branch_0_fun/all_to_all | solution.py:211
  146.4 0.0 copy-start.3
  146.4 1.9 %place.3.after_ref = f32[216,4,128]{2,1,0:T(4,128)} custom-call(s32[281]{0:T(512)S(1)} %get-tuple-element.36.plan_ref, f32[16,18,4,128]{3,2,1,0:T(4,128)S(1)} %all-to-all-done.3.back_ref), custom_call_target="tpu_custom_call" | custom-call | bytes 1000000 | tf_op jit(solution)/shard_map/cond/branch_0_fun/place/pallas_call | solution.py:294
  148.3 0.0 collective-permute-done.3.refs_1_
  148.4 0.0 collective-permute-done.4.refs_2_
  148.4 0.0 collective-permute-done.5.refs_3_
  148.4 0.0 copy-done.3
  148.4 2.6 %factors.3 = (f32[3,128,512]{2,1,0:T(8,128)}, f32[3,128,512]{2,1,0:T(8,128)}) custom-call(s32[281]{0:T(512)S(1)} %get-tuple-element.36.plan_ref, f32[216,4,128]{2,1,0:T(4,128)} %place.3.after_ref, f32[3,128,512]{2,1,0:T(8,128)S(1)} %copy-done.3, f32[3,128,512]{2,1,0:T(8,128)} %get-tuple-element.48.right_ref, ...), custom_call_target="tpu_custom_call" | custom-call | bytes 5000000 | tf_op jit(solution)/shard_map/cond/branch_0_fun/factors/pallas_call | solution.py:297
Async XLA Ops:
  0.6 5.7 %copy-start.6 = (bf16[3,128,512]{2,1,0:T(8,128)(2,1)S(1)}, bf16[3,128,512]{2,1,0:T(8,128)(2,1)}, u32[]{:S(2)}) copy-start(bf16[3,128,512]{2,1,0:T(8,128)(2,1)} %param.17) | copy-start | bytes 1179652
  6.4 15.4 %copy-start.7 = (bf16[3,512,128]{2,1,0:T(8,128)(2,1)S(1)}, bf16[3,512,128]{2,1,0:T(8,128)(2,1)}, u32[]{:S(2)}) copy-start(bf16[3,512,128]{2,1,0:T(8,128)(2,1)} %get-tuple-element.39.right_ref) | copy-start | bytes 1179652 | tf_op jit(solution)/shard_map/cond
  6.4 46.7 %all-to-all-start = ((f32[16,18,4,128]{3,2,1,0:T(4,128)}), f32[16,18,4,128]{3,2,1,0:T(4,128)S(1)}, u32[]{:S(2)}, u32[]{:S(2)}) async-start(f32[16,18,4,128]{3,2,1,0:T(4,128)} %get-tuple-element.37), calls=%async_computation | async-start | bytes 1179648 | tf_op jit(solution)/shard_map/cond/branch_0_fun/all_to_all | solution.py:211
  22.4 16.9 %collective-permute-start = (f32[8,128,128]{2,1,0:T(8,128)S(1)}, f32[8,128,128]{2,1,0:T(8,128)S(1)}, u32[]{:S(2)}, u32[]{:S(2)}) collective-permute-start(f32[8,128,128]{2,1,0:T(8,128)S(1)} %get-tuple-element.41), channel_id=1, source_target_pairs={{0,1},{1,2},{2,3},{3,0},{4,5},{5,6},{6,7},{7,4},{8,9},{9,10},{10,1... | collective-permute-start | bytes 1572872 | tf_op jit(solution)/shard_map/cond/branch_0_fun/ppermute | solution.py:217
  25.9 25.2 %collective-permute-start.1 = (f32[8,128,128]{2,1,0:T(8,128)S(1)}, f32[8,128,128]{2,1,0:T(8,128)S(1)}, u32[]{:S(2)}, u32[]{:S(2)}) collective-permute-start(f32[8,128,128]{2,1,0:T(8,128)S(1)} %get-tuple-element.42), channel_id=1, source_target_pairs={{0,2},{1,3},{2,0},{3,1},{4,6},{5,7},{6,4},{7,5},{8,10},{9,11},{10,... | collective-permute-start | bytes 1572872 | tf_op jit(solution)/shard_map/cond/branch_0_fun/ppermute | solution.py:217
  30.8 21.7 %collective-permute-start.2 = (f32[8,128,128]{2,1,0:T(8,128)S(1)}, f32[8,128,128]{2,1,0:T(8,128)S(1)}, u32[]{:S(2)}, u32[]{:S(2)}) collective-permute-start(f32[8,128,128]{2,1,0:T(8,128)S(1)} %get-tuple-element.43), channel_id=1, source_target_pairs={{0,3},{1,0},{2,1},{3,2},{4,7},{5,4},{6,5},{7,6},{8,11},{9,8},{10,9... | collective-permute-start | bytes 1572872 | tf_op jit(solution)/shard_map/cond/branch_0_fun/ppermute | solution.py:217
  81.4 4.1 %copy-start = (f32[64,8,512]{2,1,0:T(8,128)S(1)}, f32[64,8,512]{2,1,0:T(8,128)}, u32[]{:S(2)}) copy-start(f32[64,8,512]{2,1,0:T(8,128)} %get-tuple-element.45.block_ref) | copy-start | bytes 3145732 | tf_op jit(solution)/shard_map/cond
  81.4 21.2 %all-to-all-start.2 = ((f32[32,16,4,128]{3,2,1,0:T(4,128)}), f32[32,16,4,128]{3,2,1,0:T(4,128)S(1)}, u32[]{:S(2)}, u32[]{:S(2)}) async-start(f32[32,16,4,128]{3,2,1,0:T(4,128)} %bitcast.2), calls=%async_computation.2 | async-start | bytes 2097152 | tf_op jit(solution)/shard_map/cond/branch_0_fun/all_to_all | solution.py:211
  104.1 42.3 %all-to-all-start.3 = ((f32[16,18,4,128]{3,2,1,0:T(4,128)}), f32[16,18,4,128]{3,2,1,0:T(4,128)S(1)}, u32[]{:S(2)}, u32[]{:S(2)}) async-start(f32[16,18,4,128]{3,2,1,0:T(4,128)} %backward.3), calls=%async_computation.3 | async-start | bytes 1179648 | tf_op jit(solution)/shard_map/cond/branch_0_fun/all_to_all | solution.py:211
  115.4 32.9 %collective-permute-start.3 = (f32[2,128,512]{2,1,0:T(8,128)}, f32[2,128,512]{2,1,0:T(8,128)S(1)}, u32[]{:S(2)}, u32[]{:S(2)}) collective-permute-start(f32[2,128,512]{2,1,0:T(8,128)} %get-tuple-element.49), channel_id=1, source_target_pairs={{0,1},{1,2},{2,3},{3,0},{4,5},{5,6},{6,7},{7,4},{8,9},{9,10},{10,1... | collective-permute-start | bytes 1572872 | tf_op jit(solution)/shard_map/cond/branch_0_fun/ppermute | solution.py:217
  117.4 31.0 %collective-permute-start.4 = (f32[2,128,512]{2,1,0:T(8,128)}, f32[2,128,512]{2,1,0:T(8,128)S(1)}, u32[]{:S(2)}, u32[]{:S(2)}) collective-permute-start(f32[2,128,512]{2,1,0:T(8,128)} %get-tuple-element.50), channel_id=1, source_target_pairs={{0,2},{1,3},{2,0},{3,1},{4,6},{5,7},{6,4},{7,5},{8,10},{9,11},{10,... | collective-permute-start | bytes 1572872 | tf_op jit(solution)/shard_map/cond/branch_0_fun/ppermute | solution.py:217
  122.0 26.3 %collective-permute-start.5 = (f32[2,128,512]{2,1,0:T(8,128)S(1)}, f32[2,128,512]{2,1,0:T(8,128)S(1)}, u32[]{:S(2)}, u32[]{:S(2)}) collective-permute-start(f32[2,128,512]{2,1,0:T(8,128)S(1)} %get-tuple-element.51), channel_id=1, source_target_pairs={{0,3},{1,0},{2,1},{3,2},{4,7},{5,4},{6,5},{7,6},{8,11},{9,8},{10,9... | collective-permute-start | bytes 1572872 | tf_op jit(solution)/shard_map/cond/branch_0_fun/ppermute | solution.py:217
  146.4 1.9 %copy-start.3 = (f32[3,128,512]{2,1,0:T(8,128)S(1)}, f32[3,128,512]{2,1,0:T(8,128)}, u32[]{:S(2)}) copy-start(f32[3,128,512]{2,1,0:T(8,128)} %get-tuple-element.47.left_ref) | copy-start | bytes 2359300 | tf_op jit(solution)/shard_map/cond

commit v2 on v1

--- a/solution.py
+++ b/solution.py
@@ -101,17 +101,6 @@
             copy.wait()
 
 
-def place_kernel(plan_ref, back_ref, out_ref):
-    bits = log2(STRIDE)
-
-    def step(t, carry):
-        code = plan_ref[t]
-        out_ref[t] = back_ref[code >> bits, code & (STRIDE - 1)]
-        return carry
-
-    lax.fori_loop(0, out_ref.shape[0], step, 0, unroll=8)
-
-
 def forward_kernel(cap, blocks, plan_ref, in_ref, *refs):
     out_ref = refs[-1]
     planes, y_size = out_ref.shape[:2]
@@ -154,16 +143,21 @@
     return lax.dot_general(a, b, (((a_dim,), (b_dim,)), ((), ())), preferred_element_type=F32)
 
 
-def direction_kernel(plan_ref, in_ref, *refs):
-    x_size, core_size, parts, z_size, rows, width = in_ref.shape
-    pieces, (out_ref, block_ref, left_ref, right_ref, result_ref) = refs[:parts], refs[parts:]
-    side = parts * width
+def tiles(shape):
+    x_size, core_size, parts, z_size, rows, width = shape
     for x in range(x_size):
         for c in range(core_size):
             for q in range(parts):
-                block_ref[
-                    x * z_size : (x + 1) * z_size, c * rows : (c + 1) * rows, q * width : (q + 1) * width
-                ] = in_ref[x, c, q]
+                spot = (slice(x * z_size, (x + 1) * z_size), slice(c * rows, (c + 1) * rows))
+                yield (x, c, q), spot + (slice(q * width, (q + 1) * width),)
+
+
+def direction_kernel(plan_ref, in_ref, *refs):
+    parts, width = in_ref.shape[2], in_ref.shape[5]
+    pieces, (out_ref, block_ref, left_ref, right_ref, result_ref) = refs[:parts], refs[parts:]
+    side = parts * width
+    for part, spot in tiles(in_ref.shape):
+        block_ref[spot] = in_ref[part]
     for d, piece in enumerate(pieces):
         q = around(plan_ref[plan_ref.shape[0] - 1] - d, parts)
         for j in range(parts):
@@ -175,19 +169,17 @@
     high, low = split(product)
     left = left_ref[...]
     result_ref[...] = (dot(left, high, 1, 0) + dot(left, low, 1, 0)).reshape(result_ref.shape)
-    for x in range(x_size):
-        for c in range(core_size):
-            for q in range(parts):
-                out_ref[x, c, q] = result_ref[
-                    x * z_size : (x + 1) * z_size, c * rows : (c + 1) * rows, q * width : (q + 1) * width
-                ]
-
-
-def grams_kernel(plan_ref, block_ref, *refs):
-    out_refs, gram_ref = refs[:-1], refs[-1]
+    for part, spot in tiles(in_ref.shape):
+        out_ref[part] = result_ref[spot]
+
+
+def grams_kernel(plan_ref, in_ref, after_ref, *refs):
+    out_refs, (block_ref, gram_ref) = refs[:-2], refs[-2:]
     parts = len(out_refs)
     quarter = out_refs[0].shape[1]
     side = block_ref.shape[2]
+    for part, spot in tiles(in_ref.shape):
+        block_ref[spot] = in_ref[part]
     high, low = split(block_ref[...].reshape(side, side))
     for i, dim in enumerate((1, 0)):
         gram_ref[i] = dot(high, high, dim, dim) + (dot(high, low, dim, dim) + dot(low, high, dim, dim))
@@ -196,15 +188,43 @@
         out_ref[...] = gram_ref[:, pl.ds(q * quarter, quarter), :]
 
 
-def factors_kernel(plan_ref, after_ref, left_ref, right_ref, *refs):
-    pieces, (left_out, right_out) = refs[:-2], refs[-2:]
-    for d, piece in enumerate(pieces):
-        s = around(plan_ref[plan_ref.shape[0] - 1] - d, len(pieces))
-
-        @pl.when(s < left_ref.shape[0])
-        def _():
-            left_out[s] = BETA * left_ref[s] + (1.0 - BETA) * piece[0]
-            right_out[s] = BETA * right_ref[s] + (1.0 - BETA) * piece[1]
+def finish_kernel(plan_ref, back_ref, left_hbm, right_hbm, *refs):
+    parts = len(refs) - 7
+    pieces, refs = refs[:parts], refs[parts:]
+    placed_hbm, left_out, right_out, placed_ref, left_ref, right_ref, sems = refs
+    blocks = placed_ref.shape[0]
+    bits = log2(STRIDE)
+    loads = [
+        pltpu.make_async_copy(left_hbm, left_ref, sems.at[0]),
+        pltpu.make_async_copy(right_hbm, right_ref, sems.at[1]),
+    ]
+    for copy in loads:
+        copy.start()
+
+    def step(t, carry):
+        code = plan_ref[t]
+        placed_ref[t] = back_ref[code >> bits, code & (STRIDE - 1)]
+        return carry
+
+    lax.fori_loop(0, blocks, step, 0, unroll=8)
+    stores = [
+        pltpu.make_async_copy(placed_ref, placed_hbm, sems.at[2]),
+        pltpu.make_async_copy(left_ref, left_out, sems.at[3]),
+        pltpu.make_async_copy(right_ref, right_out, sems.at[4]),
+    ]
+    stores[0].start()
+    for i, ref in enumerate((left_ref, right_ref)):
+        loads[i].wait()
+        for d, piece in enumerate(pieces):
+            s = around(plan_ref[plan_ref.shape[0] - 1] - d, parts)
+
+            @pl.when(s < ref.shape[0])
+            def _():
+                ref[s] = BETA * ref[s] + (1.0 - BETA) * piece[i]
+
+        stores[1 + i].start()
+    for copy in stores:
+        copy.wait()
 
 
 def exchange(value, axes):
@@ -229,6 +249,7 @@
     send = sends[index]
     _, capacity, rows, width = send.shape
     cube = side * side * side * 2
+    any_spec = pl.BlockSpec(memory_space=pl.ANY)
 
     roots = spread(
         call(
@@ -250,23 +271,23 @@
     )(plan, moved, *roots)
     moved = exchange(moved.reshape(planes * y_size, z_size, rows, width), ("x", "core", "y"))
 
-    directions, block = call(
+    moved = moved.reshape(x_size, core_size, y_size, z_size, rows, width)
+    whole = pltpu.VMEM((x_size * z_size, core_size * rows, side), F32)
+    directions = call(
         direction_kernel,
         "direction",
-        (
-            shape(x_size, core_size, y_size, z_size, rows, width),
-            pltpu.HBM((x_size * z_size, core_size * rows, side), F32),
-        ),
-        (VMEM_SPEC, VMEM_SPEC),
+        shape(*moved.shape),
+        VMEM_SPEC,
         [SMEM_SPEC, VMEM_SPEC] + [VMEM_SPEC] * y_size,
         [
+            whole,
             pltpu.VMEM((side, side), BF16),
             pltpu.VMEM((y_size, side, width), BF16),
-            pltpu.VMEM((x_size * z_size, core_size * rows, side), F32),
+            whole,
         ],
         flops=4 * cube,
         moved=6_000_000,
-    )(plan, moved.reshape(x_size, core_size, y_size, z_size, rows, width), *roots)
+    )(plan, moved, *roots)
 
     grams = spread(
         call(
@@ -274,11 +295,11 @@
             "grams",
             (shape(2, quarter, side),) * y_size,
             (VMEM_SPEC,) * y_size,
-            [SMEM_SPEC, VMEM_SPEC],
-            [pltpu.VMEM((2, side, side), F32)],
+            [SMEM_SPEC, VMEM_SPEC, any_spec],
+            [whole, pltpu.VMEM((2, side, side), F32)],
             flops=6 * cube,
             moved=5_000_000,
-        )(plan, block)
+        )(plan, moved, directions)
     )
     back = exchange(directions.reshape(planes * y_size, z_size, rows, width), ("x", "core", "y"))
     back = call(
@@ -290,20 +311,16 @@
     )(plan, back.reshape(planes, y_size, z_size, rows, width), grams[0])
     back = exchange(back, "z")
 
-    result = pltpu.HBM((blocks, rows, width), F32)
-    placed = call(place_kernel, "place", result, VMEM_SPEC, [SMEM_SPEC, VMEM_SPEC])(
-        plan, back
-    )
-    left_new, right_new = call(
-        factors_kernel,
-        "factors",
-        (shape(*left_factor.shape), shape(*right_factor.shape)),
-        (VMEM_SPEC, VMEM_SPEC),
-        [SMEM_SPEC, pl.BlockSpec(memory_space=pl.ANY)] + [VMEM_SPEC] * (2 + y_size),
-        moved=5_000_000,
-    )(plan, placed, left_factor, right_factor, *grams)
-
-    return placed, left_new, right_new
+    factor = pltpu.VMEM(left_factor.shape, F32)
+    return call(
+        finish_kernel,
+        "finish",
+        (shape(blocks, rows, width), shape(*left_factor.shape), shape(*right_factor.shape)),
+        (any_spec,) * 3,
+        [SMEM_SPEC, VMEM_SPEC, any_spec, any_spec] + [VMEM_SPEC] * y_size,
+        [pltpu.VMEM((blocks, rows, width), F32), factor, factor, pltpu.SemaphoreType.DMA((5,))],
+        moved=6_000_000,
+    )(plan, back, left_factor, right_factor, *grams)
 
 
 def per_device(

time: 152 us -> 152 us (level)
    all_to_all x3, waiting for transfers between devices: 35.3 us -> 15.2 us  [exchange(): return lax.all_to_all(value, axes, split_axis=0, concat_axis=0, tiled=True)]
    ppermute x6, waiting for transfers between devices: 18.5 us -> 38.4 us  [spread(): lax.ppermute(pieces[d], 'y', turn(d))]
    pallas_call x3 -> x2, Pallas kernels: 7.75 us -> 6.29 us  [the longest x1 3.27 us: step(): call(direction_kernel, 'direction', shape(*moved.shape), VMEM_SPEC, [SMEM...]
  transfers between devices with their start and end apart: 9 -> 9, of which waited for: 6 -> 8; matrix products, arithmetic and copies ran while one was open for 0% -> 0% of each run, Pallas kernels for 4% -> 3%
where the time goes in v2:
time: 152 us; the launch traced here: 150 us
  waiting for transfers between devices  53.6 us (35%)
  starting transfers between devices  52.1 us (34%)
  blocking collectives  24.4 us (16%)
  Pallas kernels  18 us (12%)
    ppermute x6, waiting for transfers between devices, spread(): lax.ppermute(pieces[d], 'y', turn(d))  38.4 us
    all_to_all x3, starting transfers between devices, exchange(): return lax.all_to_all(value, axes, split_axis=0, concat_axis=0, tiled=True)  30.6 us
    all_to_all x1, blocking collectives, exchange(): return lax.all_to_all(value, axes, split_axis=0, concat_axis=0, tiled=True)  24.4 us
    ppermute x6, starting transfers between devices, spread(): lax.ppermute(pieces[d], 'y', turn(d))  21.4 us
    all_to_all x3, waiting for transfers between devices, exchange(): return lax.all_to_all(value, axes, split_axis=0, concat_axis=0, tiled=True)  15.2 us
    pallas_call x1, Pallas kernels, per_device(): call(functools.partial(select_kernel, sizes), 'select', tuple((shape(z_si...  5.04 us
    pallas_call x1, Pallas kernels, step(): call(grams_kernel, 'grams', (shape(2, quarter, side),) * y_size, (VMEM_SP...  3.7 us
    pallas_call x1, Pallas kernels, step(): call(direction_kernel, 'direction', shape(*moved.shape), VMEM_SPEC, [SMEM...  3.27 us
  transfers between devices with their start and end apart: 9, of which 8 were waited for; matrix products, arithmetic and copies ran while one was open for 0% of the time, Pallas kernels for 3%

profile of v2, /device:TPU:32, one launch (start us, length us, event | category | flops | bytes accessed | tf_op | source)
XLA Modules:
  0.0 149.9 jit_solution(3585245295141962724)
XLA Ops:
  0.6 0.0 copy-start.12
  0.6 5.0 %select.1 = (f32[16,18,4,128]{3,2,1,0:T(4,128)}, f32[16,20,4,128]{3,2,1,0:T(4,128)}, f32[16,24,4,128]{3,2,1,0:T(4,128)}, s32[281]{0:T(512)S(1)}, s32[1]{0:T(128)}) custom-call(s32[216]{0:T(256)} %owner_hbm.1, s32[216]{0:T(256)} %slab_hbm.1, s32[216]{0:T(256)} %col_hbm.1, f32[216,4,128]{2,1,0:T(4,128)} %bitcast.31), custom_call_target="tpu_custom_call" | custom-call | bytes 3000000 | tf_op jit(solution)/shard_map/select/pallas_call | solution.py:341
  6.3 0.0 copy-done.12
  6.3 143.4 %conditional.1 = ((f32[216,4,128]{2,1,0:T(4,128)}, f32[3,128,512]{2,1,0:T(8,128)}, f32[3,128,512]{2,1,0:T(8,128)})) conditional(s32[]{:T(128)} %bitcast.14, (f32[16,18,4,128]{3,2,1,0:T(4,128)}, s32[281]{0:T(512)S(1)}, bf16[3,128,512]{2,1,0:T(8,128)(2,1)S(1)}, bf16[3,512,128]{2,1,0:T(8,128)(2,1)}, f32[3,128,512]{2,1,0:T(8,128)}, ...), branch_computations={%region_0.0_spmd, %region_1.0_spmd, %region_2.0_spmd} | conditional | flops 2684354560 | bytes 52506340 | solution.py:359
  6.4 0.0 copy-start.13
  6.4 15.4 %all-to-all-start = ((f32[16,18,4,128]{3,2,1,0:T(4,128)}), f32[16,18,4,128]{3,2,1,0:T(4,128)S(1)}, u32[]{:S(2)}, u32[]{:S(2)}) async-start(f32[16,18,4,128]{3,2,1,0:T(4,128)} %get-tuple-element.37), calls=%async_computation | async-start | bytes 1179648 | tf_op jit(solution)/shard_map/cond/branch_0_fun/all_to_all | solution.py:231
  21.7 0.0 copy-done.13
  21.7 0.7 roots.3
  22.4 3.5 %collective-permute-start = (f32[8,128,128]{2,1,0:T(8,128)S(1)}, f32[8,128,128]{2,1,0:T(8,128)S(1)}, u32[]{:S(2)}, u32[]{:S(2)}) collective-permute-start(f32[8,128,128]{2,1,0:T(8,128)S(1)} %get-tuple-element.41), channel_id=1, source_target_pairs={{0,1},{1,2},{2,3},{3,0},{4,5},{5,6},{6,7},{7,4},{8,9},{9,10},{10,1... | collective-permute-start | bytes 1572872 | tf_op jit(solution)/shard_map/cond/branch_0_fun/ppermute | solution.py:237
  25.9 4.8 %collective-permute-start.1 = (f32[8,128,128]{2,1,0:T(8,128)S(1)}, f32[8,128,128]{2,1,0:T(8,128)S(1)}, u32[]{:S(2)}, u32[]{:S(2)}) collective-permute-start(f32[8,128,128]{2,1,0:T(8,128)S(1)} %get-tuple-element.42), channel_id=1, source_target_pairs={{0,2},{1,3},{2,0},{3,1},{4,6},{5,7},{6,4},{7,5},{8,10},{9,11},{10,... | collective-permute-start | bytes 1572872 | tf_op jit(solution)/shard_map/cond/branch_0_fun/ppermute | solution.py:237
  30.8 3.3 %collective-permute-start.2 = (f32[8,128,128]{2,1,0:T(8,128)S(1)}, f32[8,128,128]{2,1,0:T(8,128)S(1)}, u32[]{:S(2)}, u32[]{:S(2)}) collective-permute-start(f32[8,128,128]{2,1,0:T(8,128)S(1)} %get-tuple-element.43), channel_id=1, source_target_pairs={{0,3},{1,0},{2,1},{3,2},{4,7},{5,4},{6,5},{7,6},{8,11},{9,8},{10,9... | collective-permute-start | bytes 1572872 | tf_op jit(solution)/shard_map/cond/branch_0_fun/ppermute | solution.py:237
  34.0 5.3 %collective-permute-done.refs_1_ = f32[8,128,128]{2,1,0:T(8,128)S(1)} collective-permute-done((f32[8,128,128]{2,1,0:T(8,128)S(1)}, f32[8,128,128]{2,1,0:T(8,128)S(1)}, u32[]{:S(2)}, u32[]{:S(2)}) %collective-permute-start) | collective-permute-done | bytes 524320 | tf_op jit(solution)/shard_map/cond/branch_0_fun/ppermute | solution.py:237
  39.3 11.8 %collective-permute-done.1.refs_2_ = f32[8,128,128]{2,1,0:T(8,128)S(1)} collective-permute-done((f32[8,128,128]{2,1,0:T(8,128)S(1)}, f32[8,128,128]{2,1,0:T(8,128)S(1)}, u32[]{:S(2)}, u32[]{:S(2)}) %collective-permute-start.1) | collective-permute-done | bytes 524320 | tf_op jit(solution)/shard_map/cond/branch_0_fun/ppermute | solution.py:237
  51.1 0.0 copy-start
  51.1 1.4 collective-permute-done.2.refs_3_
  52.5 0.0 copy-start.6
  52.5 0.6 all-to-all-done.in_ref
  53.1 0.8 forward.3
  53.9 0.0 copy-done
  53.9 0.0 copy-done.6
  53.9 0.0 copy-start.1
  53.9 0.0 copy-start.7
  53.9 24.4 %all_to_all.48 = f32[32,16,4,128]{3,2,1,0:T(4,128)S(1)} all-to-all(f32[32,16,4,128]{3,2,1,0:T(4,128)S(1)} %bitcast.19), channel_id=1, replica_groups=mesh['x'=4,'z'=16,'core'=2,'y'=4] {'x','core','y'}, dimensions={0} | all-to-all | bytes 2097152 | tf_op jit(solution)/shard_map/cond/branch_0_fun/all_to_all | solution.py:231
  78.3 0.0 copy-done.1
  78.3 0.0 copy-done.7
  78.3 3.3 %direction.3.after_ref = f32[4,2,4,16,4,128]{5,4,3,2,1,0:T(4,128)} custom-call(s32[281]{0:T(512)S(1)} %get-tuple-element.36.plan_ref, f32[4,2,4,16,4,128]{5,4,3,2,1,0:T(4,128)S(1)} %bitcast.25, f32[8,128,128]{2,1,0:T(8,128)S(1)} %get-tuple-element.40.refs_0_, f32[8,128,128]{2,1,0:T(8,128)S(1)} %collective-permute-done.refs_1_, f32[8,128,128]{2,1,0:T(8,128)S(1)} %copy-done.1, ...), custom_call_target="tpu_custom_call" | custom-call | flops 1073741824 | bytes 6000000 | tf_op jit(solution)/shard_map/cond/branch_0_fun/direction/pallas_call | solution.py:276
  81.6 3.9 %all-to-all-start.2 = ((f32[32,16,4,128]{3,2,1,0:T(4,128)}), f32[32,16,4,128]{3,2,1,0:T(4,128)S(1)}, u32[]{:S(2)}, u32[]{:S(2)}) async-start(f32[32,16,4,128]{3,2,1,0:T(4,128)} %bitcast.2), calls=%async_computation.2 | async-start | bytes 2097152 | tf_op jit(solution)/shard_map/cond/branch_0_fun/all_to_all | solution.py:231
  85.5 3.7 %grams.3 = (f32[2,128,512]{2,1,0:T(8,128)S(1)}, f32[2,128,512]{2,1,0:T(8,128)}, f32[2,128,512]{2,1,0:T(8,128)}, f32[2,128,512]{2,1,0:T(8,128)S(1)}) custom-call(s32[281]{0:T(512)S(1)} %get-tuple-element.36.plan_ref, f32[4,2,4,16,4,128]{5,4,3,2,1,0:T(4,128)S(1)} %bitcast.26, f32[4,2,4,16,4,128]{5,4,3,2,1,0:T(4,128)} %direction.3.after_ref), custom_call_target="tpu_custom_call" | custom-call | flops 1610612736 | bytes 5000000 | tf_op jit(solution)/shard_map/cond/branch_0_fun/grams/pallas_call | solution.py:293
  89.2 13.4 %all-to-all-done.2 = f32[32,16,4,128]{3,2,1,0:T(4,128)S(1)} async-done(((f32[32,16,4,128]{3,2,1,0:T(4,128)}), f32[32,16,4,128]{3,2,1,0:T(4,128)S(1)}, u32[]{:S(2)}, u32[]{:S(2)}) %all-to-all-start.2) | async-done | bytes 1048608 | tf_op jit(solution)/shard_map/cond/branch_0_fun/all_to_all | solution.py:231
  102.6 1.5 %backward.3 = f32[16,18,4,128]{3,2,1,0:T(4,128)} custom-call(s32[281]{0:T(512)S(1)} %get-tuple-element.36.plan_ref, f32[8,4,16,4,128]{4,3,2,1,0:T(4,128)S(1)} %bitcast.22, f32[2,128,512]{2,1,0:T(8,128)S(1)} %get-tuple-element.44.after_ref.refs_0_), custom_call_target="tpu_custom_call" | custom-call | bytes 1000000 | tf_op jit(solution)/shard_map/cond/branch_0_fun/backward/pallas_call | solution.py:305
  104.1 11.4 %all-to-all-start.3 = ((f32[16,18,4,128]{3,2,1,0:T(4,128)}), f32[16,18,4,128]{3,2,1,0:T(4,128)S(1)}, u32[]{:S(2)}, u32[]{:S(2)}) async-start(f32[16,18,4,128]{3,2,1,0:T(4,128)} %backward.3), calls=%async_computation.3 | async-start | bytes 1179648 | tf_op jit(solution)/shard_map/cond/branch_0_fun/all_to_all | solution.py:231
  115.5 1.9 %collective-permute-start.3 = (f32[2,128,512]{2,1,0:T(8,128)}, f32[2,128,512]{2,1,0:T(8,128)S(1)}, u32[]{:S(2)}, u32[]{:S(2)}) collective-permute-start(f32[2,128,512]{2,1,0:T(8,128)} %get-tuple-element.47), channel_id=1, source_target_pairs={{0,1},{1,2},{2,3},{3,0},{4,5},{5,6},{6,7},{7,4},{8,9},{9,10},{10,1... | collective-permute-start | bytes 1572872 | tf_op jit(solution)/shard_map/cond/branch_0_fun/ppermute | solution.py:237
  117.4 4.6 %collective-permute-start.4 = (f32[2,128,512]{2,1,0:T(8,128)}, f32[2,128,512]{2,1,0:T(8,128)S(1)}, u32[]{:S(2)}, u32[]{:S(2)}) collective-permute-start(f32[2,128,512]{2,1,0:T(8,128)} %get-tuple-element.48), channel_id=1, source_target_pairs={{0,2},{1,3},{2,0},{3,1},{4,6},{5,7},{6,4},{7,5},{8,10},{9,11},{10,... | collective-permute-start | bytes 1572872 | tf_op jit(solution)/shard_map/cond/branch_0_fun/ppermute | solution.py:237
  122.0 3.3 %collective-permute-start.5 = (f32[2,128,512]{2,1,0:T(8,128)S(1)}, f32[2,128,512]{2,1,0:T(8,128)S(1)}, u32[]{:S(2)}, u32[]{:S(2)}) collective-permute-start(f32[2,128,512]{2,1,0:T(8,128)S(1)} %get-tuple-element.49), channel_id=1, source_target_pairs={{0,3},{1,0},{2,1},{3,2},{4,7},{5,4},{6,5},{7,6},{8,11},{9,8},{10,9... | collective-permute-start | bytes 1572872 | tf_op jit(solution)/shard_map/cond/branch_0_fun/ppermute | solution.py:237
  125.4 17.4 %collective-permute-done.3.refs_1_ = f32[2,128,512]{2,1,0:T(8,128)S(1)} collective-permute-done((f32[2,128,512]{2,1,0:T(8,128)}, f32[2,128,512]{2,1,0:T(8,128)S(1)}, u32[]{:S(2)}, u32[]{:S(2)}) %collective-permute-start.3) | collective-permute-done | bytes 524320 | tf_op jit(solution)/shard_map/cond/branch_0_fun/ppermute | solution.py:237
  142.7 0.0 collective-permute-done.4.refs_2_
  142.7 2.5 %collective-permute-done.5.refs_3_ = f32[2,128,512]{2,1,0:T(8,128)S(1)} collective-permute-done((f32[2,128,512]{2,1,0:T(8,128)S(1)}, f32[2,128,512]{2,1,0:T(8,128)S(1)}, u32[]{:S(2)}, u32[]{:S(2)}) %collective-permute-start.5) | collective-permute-done | bytes 524320 | tf_op jit(solution)/shard_map/cond/branch_0_fun/ppermute | solution.py:237
  145.3 1.2 all-to-all-done.3.back_ref
  146.5 3.0 %finish.3 = (f32[216,4,128]{2,1,0:T(4,128)}, f32[3,128,512]{2,1,0:T(8,128)}, f32[3,128,512]{2,1,0:T(8,128)}) custom-call(s32[281]{0:T(512)S(1)} %get-tuple-element.36.plan_ref, f32[16,18,4,128]{3,2,1,0:T(4,128)S(1)} %all-to-all-done.3.back_ref, f32[3,128,512]{2,1,0:T(8,128)} %get-tuple-element.45.left_hbm, f32[3,128,512]{2,1,0:T(8,128)} %get-tuple-element.46.right_hbm, ...), custom_call_target="tpu_custom_call" | custom-call | bytes 6000000 | tf_op jit(solution)/shard_map/cond/branch_0_fun/finish/pallas_call | solution.py:315
Async XLA Ops:
  0.6 5.7 %copy-start.12 = (bf16[3,128,512]{2,1,0:T(8,128)(2,1)S(1)}, bf16[3,128,512]{2,1,0:T(8,128)(2,1)}, u32[]{:S(2)}) copy-start(bf16[3,128,512]{2,1,0:T(8,128)(2,1)} %param.17) | copy-start | bytes 1179652
  6.4 15.4 %copy-start.13 = (bf16[3,512,128]{2,1,0:T(8,128)(2,1)S(1)}, bf16[3,512,128]{2,1,0:T(8,128)(2,1)}, u32[]{:S(2)}) copy-start(bf16[3,512,128]{2,1,0:T(8,128)(2,1)} %get-tuple-element.39.right_ref) | copy-start | bytes 1179652 | tf_op jit(solution)/shard_map/cond
  6.4 46.7 %all-to-all-start = ((f32[16,18,4,128]{3,2,1,0:T(4,128)}), f32[16,18,4,128]{3,2,1,0:T(4,128)S(1)}, u32[]{:S(2)}, u32[]{:S(2)}) async-start(f32[16,18,4,128]{3,2,1,0:T(4,128)} %get-tuple-element.37), calls=%async_computation | async-start | bytes 1179648 | tf_op jit(solution)/shard_map/cond/branch_0_fun/all_to_all | solution.py:231
  22.4 16.9 %collective-permute-start = (f32[8,128,128]{2,1,0:T(8,128)S(1)}, f32[8,128,128]{2,1,0:T(8,128)S(1)}, u32[]{:S(2)}, u32[]{:S(2)}) collective-permute-start(f32[8,128,128]{2,1,0:T(8,128)S(1)} %get-tuple-element.41), channel_id=1, source_target_pairs={{0,1},{1,2},{2,3},{3,0},{4,5},{5,6},{6,7},{7,4},{8,9},{9,10},{10,1... | collective-permute-start | bytes 1572872 | tf_op jit(solution)/shard_map/cond/branch_0_fun/ppermute | solution.py:237
  25.9 25.2 %collective-permute-start.1 = (f32[8,128,128]{2,1,0:T(8,128)S(1)}, f32[8,128,128]{2,1,0:T(8,128)S(1)}, u32[]{:S(2)}, u32[]{:S(2)}) collective-permute-start(f32[8,128,128]{2,1,0:T(8,128)S(1)} %get-tuple-element.42), channel_id=1, source_target_pairs={{0,2},{1,3},{2,0},{3,1},{4,6},{5,7},{6,4},{7,5},{8,10},{9,11},{10,... | collective-permute-start | bytes 1572872 | tf_op jit(solution)/shard_map/cond/branch_0_fun/ppermute | solution.py:237
  30.8 21.7 %collective-permute-start.2 = (f32[8,128,128]{2,1,0:T(8,128)S(1)}, f32[8,128,128]{2,1,0:T(8,128)S(1)}, u32[]{:S(2)}, u32[]{:S(2)}) collective-permute-start(f32[8,128,128]{2,1,0:T(8,128)S(1)} %get-tuple-element.43), channel_id=1, source_target_pairs={{0,3},{1,0},{2,1},{3,2},{4,7},{5,4},{6,5},{7,6},{8,11},{9,8},{10,9... | collective-permute-start | bytes 1572872 | tf_op jit(solution)/shard_map/cond/branch_0_fun/ppermute | solution.py:237
  51.1 2.7 %copy-start = (f32[8,128,128]{2,1,0:T(8,128)}, f32[8,128,128]{2,1,0:T(8,128)S(1)}, u32[]{:S(2)}) copy-start(f32[8,128,128]{2,1,0:T(8,128)S(1)} %collective-permute-done.1.refs_2_) | copy-start | bytes 1572868 | tf_op jit(solution)/shard_map/cond
  52.5 1.4 copy-start.6
  53.9 24.4 %copy-start.1 = (f32[8,128,128]{2,1,0:T(8,128)S(1)}, f32[8,128,128]{2,1,0:T(8,128)}, u32[]{:S(2)}) copy-start(f32[8,128,128]{2,1,0:T(8,128)} %copy-done) | copy-start | bytes 1572868 | tf_op jit(solution)/shard_map/cond
  53.9 24.4 %copy-start.7 = (f32[8,128,128]{2,1,0:T(8,128)S(1)}, f32[8,128,128]{2,1,0:T(8,128)}, u32[]{:S(2)}) copy-start(f32[8,128,128]{2,1,0:T(8,128)} %copy-done.6) | copy-start | bytes 1572868 | tf_op jit(solution)/shard_map/cond
  81.6 21.0 %all-to-all-start.2 = ((f32[32,16,4,128]{3,2,1,0:T(4,128)}), f32[32,16,4,128]{3,2,1,0:T(4,128)S(1)}, u32[]{:S(2)}, u32[]{:S(2)}) async-start(f32[32,16,4,128]{3,2,1,0:T(4,128)} %bitcast.2), calls=%async_computation.2 | async-start | bytes 2097152 | tf_op jit(solution)/shard_map/cond/branch_0_fun/all_to_all | solution.py:231
  104.1 42.4 %all-to-all-start.3 = ((f32[16,18,4,128]{3,2,1,0:T(4,128)}), f32[16,18,4,128]{3,2,1,0:T(4,128)S(1)}, u32[]{:S(2)}, u32[]{:S(2)}) async-start(f32[16,18,4,128]{3,2,1,0:T(4,128)} %backward.3), calls=%async_computation.3 | async-start | bytes 1179648 | tf_op jit(solution)/shard_map/cond/branch_0_fun/all_to_all | solution.py:231
  115.5 27.3 %collective-permute-start.3 = (f32[2,128,512]{2,1,0:T(8,128)}, f32[2,128,512]{2,1,0:T(8,128)S(1)}, u32[]{:S(2)}, u32[]{:S(2)}) collective-permute-start(f32[2,128,512]{2,1,0:T(8,128)} %get-tuple-element.47), channel_id=1, source_target_pairs={{0,1},{1,2},{2,3},{3,0},{4,5},{5,6},{6,7},{7,4},{8,9},{9,10},{10,1... | collective-permute-start | bytes 1572872 | tf_op jit(solution)/shard_map/cond/branch_0_fun/ppermute | solution.py:237
  117.4 25.3 %collective-permute-start.4 = (f32[2,128,512]{2,1,0:T(8,128)}, f32[2,128,512]{2,1,0:T(8,128)S(1)}, u32[]{:S(2)}, u32[]{:S(2)}) collective-permute-start(f32[2,128,512]{2,1,0:T(8,128)} %get-tuple-element.48), channel_id=1, source_target_pairs={{0,2},{1,3},{2,0},{3,1},{4,6},{5,7},{6,4},{7,5},{8,10},{9,11},{10,... | collective-permute-start | bytes 1572872 | tf_op jit(solution)/shard_map/cond/branch_0_fun/ppermute | solution.py:237
  122.0 23.2 %collective-permute-start.5 = (f32[2,128,512]{2,1,0:T(8,128)S(1)}, f32[2,128,512]{2,1,0:T(8,128)S(1)}, u32[]{:S(2)}, u32[]{:S(2)}) collective-permute-start(f32[2,128,512]{2,1,0:T(8,128)S(1)} %get-tuple-element.49), channel_id=1, source_target_pairs={{0,3},{1,0},{2,1},{3,2},{4,7},{5,4},{6,5},{7,6},{8,11},{9,8},{10,9... | collective-permute-start | bytes 1572872 | tf_op jit(solution)/shard_map/cond/branch_0_fun/ppermute | solution.py:237

commit v3 on v2

--- a/solution.py
+++ b/solution.py
@@ -65,10 +65,10 @@
         plan_ref[blocks + s] = y_size - 1
     plan_ref[blocks + 2 * stride] = lax.axis_index("y")
     z_here = lax.axis_index("z")
-    for copy in copies:
+    for copy in copies[:3]:
         copy.wait()
 
-    def move(k, carry):
+    def assign(k, carry):
         o = owner_ref[k]
         rank = count_ref[o]
         count_ref[o] = rank + 1
@@ -81,10 +81,17 @@
         plan_ref[tile] = z * stride + spot
         slot = (x * core_size + core) * y_size + rank
         plan_ref[spot + jnp.where(z == z_here, blocks, blocks + stride)] = slot
-        pack_ref[z, spot] = grad_ref[tile]
         return carry
 
-    lax.fori_loop(0, blocks, move, 0, unroll=24)
+    lax.fori_loop(0, blocks, assign, 0, unroll=8)
+    copies[3].wait()
+
+    def move(t, carry):
+        code = plan_ref[t]
+        pack_ref[code >> log2(stride), code & (stride - 1)] = grad_ref[t]
+        return carry
+
+    lax.fori_loop(0, blocks, move, 0, unroll=8)
     most = fill_ref[0]
     for z in range(1, z_size):
         most = jnp.maximum(most, fill_ref[z])
@@ -154,7 +161,8 @@
 
 def direction_kernel(plan_ref, in_ref, *refs):
     parts, width = in_ref.shape[2], in_ref.shape[5]
-    pieces, (out_ref, block_ref, left_ref, right_ref, result_ref) = refs[:parts], refs[parts:]
+    pieces, refs = refs[:parts], refs[parts:]
+    out_hbm, block_ref, left_ref, right_ref, result_ref, out_ref, sems = refs
     side = parts * width
     for part, spot in tiles(in_ref.shape):
         block_ref[spot] = in_ref[part]
@@ -164,13 +172,26 @@
             left_ref[pl.ds(q * width, width), j * width : (j + 1) * width] = piece[j].astype(BF16)
             right_ref[q, j * width : (j + 1) * width, :] = piece[parts + j].astype(BF16)
     high, low = split(block_ref[...].reshape(side, side))
-    right = jnp.concatenate([right_ref[q] for q in range(parts)], axis=1)
-    product = dot(high, right, 1, 0) + dot(low, right, 1, 0)
-    high, low = split(product)
     left = left_ref[...]
-    result_ref[...] = (dot(left, high, 1, 0) + dot(left, low, 1, 0)).reshape(result_ref.shape)
-    for part, spot in tiles(in_ref.shape):
-        out_ref[part] = result_ref[spot]
+    half = parts // 2
+    copies = []
+    for h in range(2):
+        columns = range(h * half, (h + 1) * half)
+        right = jnp.concatenate([right_ref[q] for q in columns], axis=1)
+        product = dot(high, right, 1, 0) + dot(low, right, 1, 0)
+        result = dot(left, jnp.concatenate(split(product), axis=1), 1, 0)
+        result = result[:, : half * width] + result[:, half * width :]
+        result_ref[:, :, h * half * width : (h + 1) * half * width] = result.reshape(
+            result_ref.shape[:2] + (half * width,)
+        )
+        for part, spot in tiles(in_ref.shape):
+            if part[2] in columns:
+                out_ref[part] = result_ref[spot]
+        some = (slice(None), slice(None), pl.ds(h * half, half))
+        copies.append(pltpu.make_async_copy(out_ref.at[some], out_hbm.at[some], sems.at[h]))
+        copies[-1].start()
+    for copy in copies:
+        copy.wait()
 
 
 def grams_kernel(plan_ref, in_ref, after_ref, *refs):
@@ -277,13 +298,15 @@
         direction_kernel,
         "direction",
         shape(*moved.shape),
-        VMEM_SPEC,
+        any_spec,
         [SMEM_SPEC, VMEM_SPEC] + [VMEM_SPEC] * y_size,
         [
             whole,
             pltpu.VMEM((side, side), BF16),
             pltpu.VMEM((y_size, side, width), BF16),
             whole,
+            pltpu.VMEM(moved.shape, F32),
+            pltpu.SemaphoreType.DMA((2,)),
         ],
         flops=4 * cube,
         moved=6_000_000,

time: 152 us -> 151 us (level)
  no operation moved by 1% of the time
where the time goes in v3:
time: 151 us; the launch traced here: 150 us
  waiting for transfers between devices  53.6 us (35%)
  starting transfers between devices  52.1 us (35%)
  blocking collectives  24.4 us (16%)
  Pallas kernels  18.2 us (12%)
    ppermute x6, waiting for transfers between devices, spread(): lax.ppermute(pieces[d], 'y', turn(d))  38.4 us
    all_to_all x3, starting transfers between devices, exchange(): return lax.all_to_all(value, axes, split_axis=0, concat_axis=0, tiled=True)  30.6 us
    all_to_all x1, blocking collectives, exchange(): return lax.all_to_all(value, axes, split_axis=0, concat_axis=0, tiled=True)  24.4 us
    ppermute x6, starting transfers between devices, spread(): lax.ppermute(pieces[d], 'y', turn(d))  21.4 us
    all_to_all x3, waiting for transfers between devices, exchange(): return lax.all_to_all(value, axes, split_axis=0, concat_axis=0, tiled=True)  15.2 us
    pallas_call x1, Pallas kernels, per_device(): call(functools.partial(select_kernel, sizes), 'select', tuple((shape(z_si...  4.98 us
    pallas_call x1, Pallas kernels, step(): call(grams_kernel, 'grams', (shape(2, quarter, side),) * y_size, (VMEM_SP...  3.71 us
    pallas_call x1, Pallas kernels, step(): call(direction_kernel, 'direction', shape(*moved.shape), any_spec, [SMEM_...  3.53 us
  transfers between devices with their start and end apart: 9, of which 8 were waited for; matrix products, arithmetic and copies ran while one was open for 0% of the time, Pallas kernels for 3%

profile of v3, /device:TPU:32, one launch (start us, length us, event | category | flops | bytes accessed | tf_op | source)
XLA Modules:
  0.0 150.1 jit_solution(4855390327565930897)
XLA Ops:
  0.6 0.0 copy-start.12
  0.6 5.0 %select.1 = (f32[16,18,4,128]{3,2,1,0:T(4,128)}, f32[16,20,4,128]{3,2,1,0:T(4,128)}, f32[16,24,4,128]{3,2,1,0:T(4,128)}, s32[281]{0:T(512)S(1)}, s32[1]{0:T(128)}) custom-call(s32[216]{0:T(256)} %owner_hbm.1, s32[216]{0:T(256)} %slab_hbm.1, s32[216]{0:T(256)} %col_hbm.1, f32[216,4,128]{2,1,0:T(4,128)} %bitcast.31), custom_call_target="tpu_custom_call" | custom-call | bytes 3000000 | tf_op jit(solution)/shard_map/select/pallas_call | solution.py:364
  6.3 0.0 copy-done.12
  6.3 143.7 %conditional.1 = ((f32[216,4,128]{2,1,0:T(4,128)}, f32[3,128,512]{2,1,0:T(8,128)}, f32[3,128,512]{2,1,0:T(8,128)})) conditional(s32[]{:T(128)} %bitcast.14, (f32[16,18,4,128]{3,2,1,0:T(4,128)}, s32[281]{0:T(512)S(1)}, bf16[3,128,512]{2,1,0:T(8,128)(2,1)S(1)}, bf16[3,512,128]{2,1,0:T(8,128)(2,1)}, f32[3,128,512]{2,1,0:T(8,128)}, ...), branch_computations={%region_0.0_spmd, %region_1.0_spmd, %region_2.0_spmd} | conditional | flops 2684354560 | bytes 52506340 | solution.py:382
  6.3 0.0 copy-start.13
  6.3 15.4 %all-to-all-start = ((f32[16,18,4,128]{3,2,1,0:T(4,128)}), f32[16,18,4,128]{3,2,1,0:T(4,128)S(1)}, u32[]{:S(2)}, u32[]{:S(2)}) async-start(f32[16,18,4,128]{3,2,1,0:T(4,128)} %get-tuple-element.37), calls=%async_computation | async-start | bytes 1179648 | tf_op jit(solution)/shard_map/cond/branch_0_fun/all_to_all | solution.py:252
  21.7 0.0 copy-done.13
  21.7 0.7 roots.3
  22.4 3.5 %collective-permute-start = (f32[8,128,128]{2,1,0:T(8,128)S(1)}, f32[8,128,128]{2,1,0:T(8,128)S(1)}, u32[]{:S(2)}, u32[]{:S(2)}) collective-permute-start(f32[8,128,128]{2,1,0:T(8,128)S(1)} %get-tuple-element.41), channel_id=1, source_target_pairs={{0,1},{1,2},{2,3},{3,0},{4,5},{5,6},{6,7},{7,4},{8,9},{9,10},{10,1... | collective-permute-start | bytes 1572872 | tf_op jit(solution)/shard_map/cond/branch_0_fun/ppermute | solution.py:258
  25.9 4.8 %collective-permute-start.1 = (f32[8,128,128]{2,1,0:T(8,128)S(1)}, f32[8,128,128]{2,1,0:T(8,128)S(1)}, u32[]{:S(2)}, u32[]{:S(2)}) collective-permute-start(f32[8,128,128]{2,1,0:T(8,128)S(1)} %get-tuple-element.42), channel_id=1, source_target_pairs={{0,2},{1,3},{2,0},{3,1},{4,6},{5,7},{6,4},{7,5},{8,10},{9,11},{10,... | collective-permute-start | bytes 1572872 | tf_op jit(solution)/shard_map/cond/branch_0_fun/ppermute | solution.py:258
  30.7 3.3 %collective-permute-start.2 = (f32[8,128,128]{2,1,0:T(8,128)S(1)}, f32[8,128,128]{2,1,0:T(8,128)S(1)}, u32[]{:S(2)}, u32[]{:S(2)}) collective-permute-start(f32[8,128,128]{2,1,0:T(8,128)S(1)} %get-tuple-element.43), channel_id=1, source_target_pairs={{0,3},{1,0},{2,1},{3,2},{4,7},{5,4},{6,5},{7,6},{8,11},{9,8},{10,9... | collective-permute-start | bytes 1572872 | tf_op jit(solution)/shard_map/cond/branch_0_fun/ppermute | solution.py:258
  34.0 5.3 %collective-permute-done.refs_1_ = f32[8,128,128]{2,1,0:T(8,128)S(1)} collective-permute-done((f32[8,128,128]{2,1,0:T(8,128)S(1)}, f32[8,128,128]{2,1,0:T(8,128)S(1)}, u32[]{:S(2)}, u32[]{:S(2)}) %collective-permute-start) | collective-permute-done | bytes 524320 | tf_op jit(solution)/shard_map/cond/branch_0_fun/ppermute | solution.py:258
  39.2 11.8 %collective-permute-done.1.refs_2_ = f32[8,128,128]{2,1,0:T(8,128)S(1)} collective-permute-done((f32[8,128,128]{2,1,0:T(8,128)S(1)}, f32[8,128,128]{2,1,0:T(8,128)S(1)}, u32[]{:S(2)}, u32[]{:S(2)}) %collective-permute-start.1) | collective-permute-done | bytes 524320 | tf_op jit(solution)/shard_map/cond/branch_0_fun/ppermute | solution.py:258
  51.1 0.0 copy-start
  51.1 1.4 collective-permute-done.2.refs_3_
  52.4 0.0 copy-start.6
  52.4 0.6 all-to-all-done.in_ref
  53.0 0.8 forward.3
  53.8 0.0 copy-done
  53.8 0.0 copy-done.6
  53.8 0.0 copy-start.1
  53.8 0.0 copy-start.7
  53.9 24.4 %all_to_all.48 = f32[32,16,4,128]{3,2,1,0:T(4,128)S(1)} all-to-all(f32[32,16,4,128]{3,2,1,0:T(4,128)S(1)} %bitcast.19), channel_id=1, replica_groups=mesh['x'=4,'z'=16,'core'=2,'y'=4] {'x','core','y'}, dimensions={0} | all-to-all | bytes 2097152 | tf_op jit(solution)/shard_map/cond/branch_0_fun/all_to_all | solution.py:252
  78.2 0.0 copy-done.1
  78.2 0.0 copy-done.7
  78.2 3.5 %direction.3.after_ref = f32[4,2,4,16,4,128]{5,4,3,2,1,0:T(4,128)} custom-call(s32[281]{0:T(512)S(1)} %get-tuple-element.36.plan_ref, f32[4,2,4,16,4,128]{5,4,3,2,1,0:T(4,128)S(1)} %bitcast.25, f32[8,128,128]{2,1,0:T(8,128)S(1)} %get-tuple-element.40.refs_0_, f32[8,128,128]{2,1,0:T(8,128)S(1)} %collective-permute-done.refs_1_, f32[8,128,128]{2,1,0:T(8,128)S(1)} %copy-done.1, ...), custom_call_target="tpu_custom_call" | custom-call | flops 1073741824 | bytes 6000000 | tf_op jit(solution)/shard_map/cond/branch_0_fun/direction/pallas_call | solution.py:297
  81.8 3.9 %all-to-all-start.2 = ((f32[32,16,4,128]{3,2,1,0:T(4,128)}), f32[32,16,4,128]{3,2,1,0:T(4,128)S(1)}, u32[]{:S(2)}, u32[]{:S(2)}) async-start(f32[32,16,4,128]{3,2,1,0:T(4,128)} %bitcast.2), calls=%async_computation.2 | async-start | bytes 2097152 | tf_op jit(solution)/shard_map/cond/branch_0_fun/all_to_all | solution.py:252
  85.7 3.7 %grams.3 = (f32[2,128,512]{2,1,0:T(8,128)S(1)}, f32[2,128,512]{2,1,0:T(8,128)}, f32[2,128,512]{2,1,0:T(8,128)}, f32[2,128,512]{2,1,0:T(8,128)S(1)}) custom-call(s32[281]{0:T(512)S(1)} %get-tuple-element.36.plan_ref, f32[4,2,4,16,4,128]{5,4,3,2,1,0:T(4,128)S(1)} %bitcast.26, f32[4,2,4,16,4,128]{5,4,3,2,1,0:T(4,128)} %direction.3.after_ref), custom_call_target="tpu_custom_call" | custom-call | flops 1610612736 | bytes 5000000 | tf_op jit(solution)/shard_map/cond/branch_0_fun/grams/pallas_call | solution.py:316
  89.4 13.4 %all-to-all-done.2 = f32[32,16,4,128]{3,2,1,0:T(4,128)S(1)} async-done(((f32[32,16,4,128]{3,2,1,0:T(4,128)}), f32[32,16,4,128]{3,2,1,0:T(4,128)S(1)}, u32[]{:S(2)}, u32[]{:S(2)}) %all-to-all-start.2) | async-done | bytes 1048608 | tf_op jit(solution)/shard_map/cond/branch_0_fun/all_to_all | solution.py:252
  102.8 1.5 backward.3
  104.3 11.3 %all-to-all-start.3 = ((f32[16,18,4,128]{3,2,1,0:T(4,128)}), f32[16,18,4,128]{3,2,1,0:T(4,128)S(1)}, u32[]{:S(2)}, u32[]{:S(2)}) async-start(f32[16,18,4,128]{3,2,1,0:T(4,128)} %backward.3), calls=%async_computation.3 | async-start | bytes 1179648 | tf_op jit(solution)/shard_map/cond/branch_0_fun/all_to_all | solution.py:252
  115.7 1.9 %collective-permute-start.3 = (f32[2,128,512]{2,1,0:T(8,128)}, f32[2,128,512]{2,1,0:T(8,128)S(1)}, u32[]{:S(2)}, u32[]{:S(2)}) collective-permute-start(f32[2,128,512]{2,1,0:T(8,128)} %get-tuple-element.47), channel_id=1, source_target_pairs={{0,1},{1,2},{2,3},{3,0},{4,5},{5,6},{6,7},{7,4},{8,9},{9,10},{10,1... | collective-permute-start | bytes 1572872 | tf_op jit(solution)/shard_map/cond/branch_0_fun/ppermute | solution.py:258
  117.6 4.6 %collective-permute-start.4 = (f32[2,128,512]{2,1,0:T(8,128)}, f32[2,128,512]{2,1,0:T(8,128)S(1)}, u32[]{:S(2)}, u32[]{:S(2)}) collective-permute-start(f32[2,128,512]{2,1,0:T(8,128)} %get-tuple-element.48), channel_id=1, source_target_pairs={{0,2},{1,3},{2,0},{3,1},{4,6},{5,7},{6,4},{7,5},{8,10},{9,11},{10,... | collective-permute-start | bytes 1572872 | tf_op jit(solution)/shard_map/cond/branch_0_fun/ppermute | solution.py:258
  122.3 3.3 %collective-permute-start.5 = (f32[2,128,512]{2,1,0:T(8,128)S(1)}, f32[2,128,512]{2,1,0:T(8,128)S(1)}, u32[]{:S(2)}, u32[]{:S(2)}) collective-permute-start(f32[2,128,512]{2,1,0:T(8,128)S(1)} %get-tuple-element.49), channel_id=1, source_target_pairs={{0,3},{1,0},{2,1},{3,2},{4,7},{5,4},{6,5},{7,6},{8,11},{9,8},{10,9... | collective-permute-start | bytes 1572872 | tf_op jit(solution)/shard_map/cond/branch_0_fun/ppermute | solution.py:258
  125.6 17.4 %collective-permute-done.3.refs_1_ = f32[2,128,512]{2,1,0:T(8,128)S(1)} collective-permute-done((f32[2,128,512]{2,1,0:T(8,128)}, f32[2,128,512]{2,1,0:T(8,128)S(1)}, u32[]{:S(2)}, u32[]{:S(2)}) %collective-permute-start.3) | collective-permute-done | bytes 524320 | tf_op jit(solution)/shard_map/cond/branch_0_fun/ppermute | solution.py:258
  143.0 0.0 collective-permute-done.4.refs_2_
  143.0 2.5 %collective-permute-done.5.refs_3_ = f32[2,128,512]{2,1,0:T(8,128)S(1)} collective-permute-done((f32[2,128,512]{2,1,0:T(8,128)S(1)}, f32[2,128,512]{2,1,0:T(8,128)S(1)}, u32[]{:S(2)}, u32[]{:S(2)}) %collective-permute-start.5) | collective-permute-done | bytes 524320 | tf_op jit(solution)/shard_map/cond/branch_0_fun/ppermute | solution.py:258
  145.5 1.2 all-to-all-done.3.back_ref
  146.7 3.0 %finish.3 = (f32[216,4,128]{2,1,0:T(4,128)}, f32[3,128,512]{2,1,0:T(8,128)}, f32[3,128,512]{2,1,0:T(8,128)}) custom-call(s32[281]{0:T(512)S(1)} %get-tuple-element.36.plan_ref, f32[16,18,4,128]{3,2,1,0:T(4,128)S(1)} %all-to-all-done.3.back_ref, f32[3,128,512]{2,1,0:T(8,128)} %get-tuple-element.45.left_hbm, f32[3,128,512]{2,1,0:T(8,128)} %get-tuple-element.46.right_hbm, ...), custom_call_target="tpu_custom_call" | custom-call | bytes 6000000 | tf_op jit(solution)/shard_map/cond/branch_0_fun/finish/pallas_call | solution.py:338
Async XLA Ops:
  0.6 5.6 %copy-start.12 = (bf16[3,128,512]{2,1,0:T(8,128)(2,1)S(1)}, bf16[3,128,512]{2,1,0:T(8,128)(2,1)}, u32[]{:S(2)}) copy-start(bf16[3,128,512]{2,1,0:T(8,128)(2,1)} %param.17) | copy-start | bytes 1179652
  6.3 15.4 %copy-start.13 = (bf16[3,512,128]{2,1,0:T(8,128)(2,1)S(1)}, bf16[3,512,128]{2,1,0:T(8,128)(2,1)}, u32[]{:S(2)}) copy-start(bf16[3,512,128]{2,1,0:T(8,128)(2,1)} %get-tuple-element.39.right_ref) | copy-start | bytes 1179652 | tf_op jit(solution)/shard_map/cond
  6.3 46.7 %all-to-all-start = ((f32[16,18,4,128]{3,2,1,0:T(4,128)}), f32[16,18,4,128]{3,2,1,0:T(4,128)S(1)}, u32[]{:S(2)}, u32[]{:S(2)}) async-start(f32[16,18,4,128]{3,2,1,0:T(4,128)} %get-tuple-element.37), calls=%async_computation | async-start | bytes 1179648 | tf_op jit(solution)/shard_map/cond/branch_0_fun/all_to_all | solution.py:252
  22.4 16.9 %collective-permute-start = (f32[8,128,128]{2,1,0:T(8,128)S(1)}, f32[8,128,128]{2,1,0:T(8,128)S(1)}, u32[]{:S(2)}, u32[]{:S(2)}) collective-permute-start(f32[8,128,128]{2,1,0:T(8,128)S(1)} %get-tuple-element.41), channel_id=1, source_target_pairs={{0,1},{1,2},{2,3},{3,0},{4,5},{5,6},{6,7},{7,4},{8,9},{9,10},{10,1... | collective-permute-start | bytes 1572872 | tf_op jit(solution)/shard_map/cond/branch_0_fun/ppermute | solution.py:258
  25.9 25.2 %collective-permute-start.1 = (f32[8,128,128]{2,1,0:T(8,128)S(1)}, f32[8,128,128]{2,1,0:T(8,128)S(1)}, u32[]{:S(2)}, u32[]{:S(2)}) collective-permute-start(f32[8,128,128]{2,1,0:T(8,128)S(1)} %get-tuple-element.42), channel_id=1, source_target_pairs={{0,2},{1,3},{2,0},{3,1},{4,6},{5,7},{6,4},{7,5},{8,10},{9,11},{10,... | collective-permute-start | bytes 1572872 | tf_op jit(solution)/shard_map/cond/branch_0_fun/ppermute | solution.py:258
  30.7 21.7 %collective-permute-start.2 = (f32[8,128,128]{2,1,0:T(8,128)S(1)}, f32[8,128,128]{2,1,0:T(8,128)S(1)}, u32[]{:S(2)}, u32[]{:S(2)}) collective-permute-start(f32[8,128,128]{2,1,0:T(8,128)S(1)} %get-tuple-element.43), channel_id=1, source_target_pairs={{0,3},{1,0},{2,1},{3,2},{4,7},{5,4},{6,5},{7,6},{8,11},{9,8},{10,9... | collective-permute-start | bytes 1572872 | tf_op jit(solution)/shard_map/cond/branch_0_fun/ppermute | solution.py:258
  51.1 2.7 %copy-start = (f32[8,128,128]{2,1,0:T(8,128)}, f32[8,128,128]{2,1,0:T(8,128)S(1)}, u32[]{:S(2)}) copy-start(f32[8,128,128]{2,1,0:T(8,128)S(1)} %collective-permute-done.1.refs_2_) | copy-start | bytes 1572868 | tf_op jit(solution)/shard_map/cond
  52.4 1.4 copy-start.6
  53.8 24.4 %copy-start.1 = (f32[8,128,128]{2,1,0:T(8,128)S(1)}, f32[8,128,128]{2,1,0:T(8,128)}, u32[]{:S(2)}) copy-start(f32[8,128,128]{2,1,0:T(8,128)} %copy-done) | copy-start | bytes 1572868 | tf_op jit(solution)/shard_map/cond
  53.8 24.4 %copy-start.7 = (f32[8,128,128]{2,1,0:T(8,128)S(1)}, f32[8,128,128]{2,1,0:T(8,128)}, u32[]{:S(2)}) copy-start(f32[8,128,128]{2,1,0:T(8,128)} %copy-done.6) | copy-start | bytes 1572868 | tf_op jit(solution)/shard_map/cond
  81.8 21.1 %all-to-all-start.2 = ((f32[32,16,4,128]{3,2,1,0:T(4,128)}), f32[32,16,4,128]{3,2,1,0:T(4,128)S(1)}, u32[]{:S(2)}, u32[]{:S(2)}) async-start(f32[32,16,4,128]{3,2,1,0:T(4,128)} %bitcast.2), calls=%async_computation.2 | async-start | bytes 2097152 | tf_op jit(solution)/shard_map/cond/branch_0_fun/all_to_all | solution.py:252
  104.3 42.4 %all-to-all-start.3 = ((f32[16,18,4,128]{3,2,1,0:T(4,128)}), f32[16,18,4,128]{3,2,1,0:T(4,128)S(1)}, u32[]{:S(2)}, u32[]{:S(2)}) async-start(f32[16,18,4,128]{3,2,1,0:T(4,128)} %backward.3), calls=%async_computation.3 | async-start | bytes 1179648 | tf_op jit(solution)/shard_map/cond/branch_0_fun/all_to_all | solution.py:252
  115.7 27.3 %collective-permute-start.3 = (f32[2,128,512]{2,1,0:T(8,128)}, f32[2,128,512]{2,1,0:T(8,128)S(1)}, u32[]{:S(2)}, u32[]{:S(2)}) collective-permute-start(f32[2,128,512]{2,1,0:T(8,128)} %get-tuple-element.47), channel_id=1, source_target_pairs={{0,1},{1,2},{2,3},{3,0},{4,5},{5,6},{6,7},{7,4},{8,9},{9,10},{10,1... | collective-permute-start | bytes 1572872 | tf_op jit(solution)/shard_map/cond/branch_0_fun/ppermute | solution.py:258
  117.6 25.3 %collective-permute-start.4 = (f32[2,128,512]{2,1,0:T(8,128)}, f32[2,128,512]{2,1,0:T(8,128)S(1)}, u32[]{:S(2)}, u32[]{:S(2)}) collective-permute-start(f32[2,128,512]{2,1,0:T(8,128)} %get-tuple-element.48), channel_id=1, source_target_pairs={{0,2},{1,3},{2,0},{3,1},{4,6},{5,7},{6,4},{7,5},{8,10},{9,11},{10,... | collective-permute-start | bytes 1572872 | tf_op jit(solution)/shard_map/cond/branch_0_fun/ppermute | solution.py:258
  122.3 23.2 %collective-permute-start.5 = (f32[2,128,512]{2,1,0:T(8,128)S(1)}, f32[2,128,512]{2,1,0:T(8,128)S(1)}, u32[]{:S(2)}, u32[]{:S(2)}) collective-permute-start(f32[2,128,512]{2,1,0:T(8,128)S(1)} %get-tuple-element.49), channel_id=1, source_target_pairs={{0,3},{1,0},{2,1},{3,2},{4,7},{5,4},{6,5},{7,6},{8,11},{9,8},{10,9... | collective-permute-start | bytes 1572872 | tf_op jit(solution)/shard_map/cond/branch_0_fun/ppermute | solution.py:258

commit v4 on v2

--- a/solution.py
+++ b/solution.py
@@ -234,7 +234,9 @@
 def spread(pieces):
     size = len(pieces)
     turn = lambda d: [(i, (i + d) % size) for i in range(size)]
-    return [pieces[0]] + [lax.ppermute(pieces[d], "y", turn(d)) for d in range(1, size)]
+    far_first = sorted(range(1, size), key=lambda d: -min(d, size - d))
+    moved = {d: lax.ppermute(pieces[d], "y", turn(d)) for d in far_first}
+    return [pieces[0]] + [moved[d] for d in range(1, size)]
 
 
 def shape(*dims):

time: 152 us -> 152 us (level); the launches traced: 150 us -> 153 us
  waiting for transfers between devices: 53.6 us -> 59 us
  starting transfers between devices: 52.1 us -> 49 us
    all_to_all x3, waiting for transfers between devices: 15.2 us -> 22.3 us  [exchange(): return lax.all_to_all(value, axes, split_axis=0, concat_axis=0, tiled=True)]
    all_to_all x3, starting transfers between devices: 30.6 us -> 28.2 us  [exchange(): return lax.all_to_all(value, axes, split_axis=0, concat_axis=0, tiled=True)]
    ppermute x6, waiting for transfers between devices: 38.4 us -> 36.7 us  [spread(): moved = {d: lax.ppermute(pieces[d], 'y', turn(d)) for d in far_first}]
  transfers between devices with their start and end apart: 9 -> 9, of which waited for: 8 -> 9; matrix products, arithmetic and copies ran while one was open for 0% -> 0% of each run, Pallas kernels for 3% -> 3%
where the time goes in v4:
time: 152 us; the launch traced here: 153 us
  waiting for transfers between devices  59 us (39%)
  starting transfers between devices  49 us (32%)
  blocking collectives  24.4 us (16%)
  Pallas kernels  18.1 us (12%)
    ppermute x6, waiting for transfers between devices, spread(): moved = {d: lax.ppermute(pieces[d], 'y', turn(d)) for d in far_first}  36.7 us
    all_to_all x3, starting transfers between devices, exchange(): return lax.all_to_all(value, axes, split_axis=0, concat_axis=0, tiled=True)  28.2 us
    all_to_all x1, blocking collectives, exchange(): return lax.all_to_all(value, axes, split_axis=0, concat_axis=0, tiled=True)  24.4 us
    all_to_all x3, waiting for transfers between devices, exchange(): return lax.all_to_all(value, axes, split_axis=0, concat_axis=0, tiled=True)  22.3 us
    ppermute x6, starting transfers between devices, spread(): moved = {d: lax.ppermute(pieces[d], 'y', turn(d)) for d in far_first}  20.8 us
    pallas_call x1, Pallas kernels, per_device(): call(functools.partial(select_kernel, sizes), 'select', tuple((shape(z_si...  5.07 us
    pallas_call x1, Pallas kernels, step(): call(grams_kernel, 'grams', (shape(2, quarter, side),) * y_size, (VMEM_SP...  3.7 us
    pallas_call x1, Pallas kernels, step(): call(direction_kernel, 'direction', shape(*moved.shape), VMEM_SPEC, [SMEM...  3.28 us
  transfers between devices with their start and end apart: 9, of which 9 were waited for; matrix products, arithmetic and copies ran while one was open for 0% of the time, Pallas kernels for 3%

profile of v4, /device:TPU:32, one launch (start us, length us, event | category | flops | bytes accessed | tf_op | source)
XLA Modules:
  0.0 152.6 jit_solution(3585245295141962724)
XLA Ops:
  0.6 0.0 copy-start.12
  0.6 5.1 %select.1 = (f32[16,18,4,128]{3,2,1,0:T(4,128)}, f32[16,20,4,128]{3,2,1,0:T(4,128)}, f32[16,24,4,128]{3,2,1,0:T(4,128)}, s32[281]{0:T(512)S(1)}, s32[1]{0:T(128)}) custom-call(s32[216]{0:T(256)} %owner_hbm.1, s32[216]{0:T(256)} %slab_hbm.1, s32[216]{0:T(256)} %col_hbm.1, f32[216,4,128]{2,1,0:T(4,128)} %bitcast.31), custom_call_target="tpu_custom_call" | custom-call | bytes 3000000 | tf_op jit(solution)/shard_map/select/pallas_call | solution.py:343
  6.4 0.0 copy-done.12
  6.4 146.0 %conditional.1 = ((f32[216,4,128]{2,1,0:T(4,128)}, f32[3,128,512]{2,1,0:T(8,128)}, f32[3,128,512]{2,1,0:T(8,128)})) conditional(s32[]{:T(128)} %bitcast.14, (f32[16,18,4,128]{3,2,1,0:T(4,128)}, s32[281]{0:T(512)S(1)}, bf16[3,128,512]{2,1,0:T(8,128)(2,1)S(1)}, bf16[3,512,128]{2,1,0:T(8,128)(2,1)}, f32[3,128,512]{2,1,0:T(8,128)}, ...), branch_computations={%region_0.0_spmd, %region_1.0_spmd, %region_2.0_spmd} | conditional | flops 2684354560 | bytes 52506340 | solution.py:361
  6.4 0.0 copy-start.14
  6.4 15.4 %all-to-all-start.4 = ((f32[16,20,4,128]{3,2,1,0:T(4,128)}), f32[16,20,4,128]{3,2,1,0:T(4,128)S(1)}, u32[]{:S(2)}, u32[]{:S(2)}) async-start(f32[16,20,4,128]{3,2,1,0:T(4,128)} %get-tuple-element.51), calls=%async_computation.4 | async-start | bytes 1310720 | tf_op jit(solution)/shard_map/cond/branch_1_fun/all_to_all | solution.py:231
  21.8 0.0 copy-done.14
  21.8 0.7 roots.4
  22.5 3.5 %collective-permute-start.6 = (f32[8,128,128]{2,1,0:T(8,128)S(1)}, f32[8,128,128]{2,1,0:T(8,128)S(1)}, u32[]{:S(2)}, u32[]{:S(2)}) collective-permute-start(f32[8,128,128]{2,1,0:T(8,128)S(1)} %get-tuple-element.55), channel_id=1, source_target_pairs={{0,1},{1,2},{2,3},{3,0},{4,5},{5,6},{6,7},{7,4},{8,9},{9,10},{10,1... | collective-permute-start | bytes 1572872 | tf_op jit(solution)/shard_map/cond/branch_1_fun/ppermute | solution.py:238
  26.0 4.8 %collective-permute-start.7 = (f32[8,128,128]{2,1,0:T(8,128)S(1)}, f32[8,128,128]{2,1,0:T(8,128)S(1)}, u32[]{:S(2)}, u32[]{:S(2)}) collective-permute-start(f32[8,128,128]{2,1,0:T(8,128)S(1)} %get-tuple-element.56), channel_id=1, source_target_pairs={{0,2},{1,3},{2,0},{3,1},{4,6},{5,7},{6,4},{7,5},{8,10},{9,11},{10,... | collective-permute-start | bytes 1572872 | tf_op jit(solution)/shard_map/cond/branch_1_fun/ppermute | solution.py:238
  30.8 3.3 %collective-permute-start.8 = (f32[8,128,128]{2,1,0:T(8,128)S(1)}, f32[8,128,128]{2,1,0:T(8,128)S(1)}, u32[]{:S(2)}, u32[]{:S(2)}) collective-permute-start(f32[8,128,128]{2,1,0:T(8,128)S(1)} %get-tuple-element.57), channel_id=1, source_target_pairs={{0,3},{1,0},{2,1},{3,2},{4,7},{5,4},{6,5},{7,6},{8,11},{9,8},{10,9... | collective-permute-start | bytes 1572872 | tf_op jit(solution)/shard_map/cond/branch_1_fun/ppermute | solution.py:238
  34.1 5.3 %collective-permute-done.6.refs_1_ = f32[8,128,128]{2,1,0:T(8,128)S(1)} collective-permute-done((f32[8,128,128]{2,1,0:T(8,128)S(1)}, f32[8,128,128]{2,1,0:T(8,128)S(1)}, u32[]{:S(2)}, u32[]{:S(2)}) %collective-permute-start.6) | collective-permute-done | bytes 524320 | tf_op jit(solution)/shard_map/cond/branch_1_fun/ppermute | solution.py:238
  39.4 11.8 %collective-permute-done.7.refs_2_ = f32[8,128,128]{2,1,0:T(8,128)S(1)} collective-permute-done((f32[8,128,128]{2,1,0:T(8,128)S(1)}, f32[8,128,128]{2,1,0:T(8,128)S(1)}, u32[]{:S(2)}, u32[]{:S(2)}) %collective-permute-start.7) | collective-permute-done | bytes 524320 | tf_op jit(solution)/shard_map/cond/branch_1_fun/ppermute | solution.py:238
  51.2 0.0 copy-start.2
  51.2 1.4 collective-permute-done.8.refs_3_
  52.5 0.0 copy-start.8
  52.5 3.0 %all-to-all-done.4.in_ref = f32[16,20,4,128]{3,2,1,0:T(4,128)S(1)} async-done(((f32[16,20,4,128]{3,2,1,0:T(4,128)}), f32[16,20,4,128]{3,2,1,0:T(4,128)S(1)}, u32[]{:S(2)}, u32[]{:S(2)}) %all-to-all-start.4) | async-done | bytes 655392 | tf_op jit(solution)/shard_map/cond/branch_1_fun/all_to_all | solution.py:231
  55.6 0.8 forward.4
  56.4 0.0 copy-done.2
  56.4 0.0 copy-done.8
  56.4 0.0 copy-start.3
  56.4 0.0 copy-start.9
  56.4 24.4 %all_to_all.49 = f32[32,16,4,128]{3,2,1,0:T(4,128)S(1)} all-to-all(f32[32,16,4,128]{3,2,1,0:T(4,128)S(1)} %bitcast.20), channel_id=1, replica_groups=mesh['x'=4,'z'=16,'core'=2,'y'=4] {'x','core','y'}, dimensions={0} | all-to-all | bytes 2097152 | tf_op jit(solution)/shard_map/cond/branch_1_fun/all_to_all | solution.py:231
  80.8 0.0 copy-done.3
  80.8 0.0 copy-done.9
  80.8 3.3 %direction.4.after_ref = f32[4,2,4,16,4,128]{5,4,3,2,1,0:T(4,128)} custom-call(s32[281]{0:T(512)S(1)} %get-tuple-element.50.plan_ref, f32[4,2,4,16,4,128]{5,4,3,2,1,0:T(4,128)S(1)} %bitcast.27, f32[8,128,128]{2,1,0:T(8,128)S(1)} %get-tuple-element.54.refs_0_, f32[8,128,128]{2,1,0:T(8,128)S(1)} %collective-permute-done.6.refs_1_, ...), custom_call_target="tpu_custom_call" | custom-call | flops 1073741824 | bytes 6000000 | tf_op jit(solution)/shard_map/cond/branch_1_fun/direction/pallas_call | solution.py:278
  84.1 3.9 %all-to-all-start.6 = ((f32[32,16,4,128]{3,2,1,0:T(4,128)}), f32[32,16,4,128]{3,2,1,0:T(4,128)S(1)}, u32[]{:S(2)}, u32[]{:S(2)}) async-start(f32[32,16,4,128]{3,2,1,0:T(4,128)} %bitcast.6), calls=%async_computation.6 | async-start | bytes 2097152 | tf_op jit(solution)/shard_map/cond/branch_1_fun/all_to_all | solution.py:231
  88.0 3.7 %grams.4 = (f32[2,128,512]{2,1,0:T(8,128)S(1)}, f32[2,128,512]{2,1,0:T(8,128)S(1)}, f32[2,128,512]{2,1,0:T(8,128)}, f32[2,128,512]{2,1,0:T(8,128)}) custom-call(s32[281]{0:T(512)S(1)} %get-tuple-element.50.plan_ref, f32[4,2,4,16,4,128]{5,4,3,2,1,0:T(4,128)S(1)} %bitcast.28, f32[4,2,4,16,4,128]{5,4,3,2,1,0:T(4,128)} %direction.4.after_ref), custom_call_target="tpu_custom_call" | custom-call | flops 1610612736 | bytes 5000000 | tf_op jit(solution)/shard_map/cond/branch_1_fun/grams/pallas_call | solution.py:295
  91.7 13.4 %all-to-all-done.6 = f32[32,16,4,128]{3,2,1,0:T(4,128)S(1)} async-done(((f32[32,16,4,128]{3,2,1,0:T(4,128)}), f32[32,16,4,128]{3,2,1,0:T(4,128)S(1)}, u32[]{:S(2)}, u32[]{:S(2)}) %all-to-all-start.6) | async-done | bytes 1048608 | tf_op jit(solution)/shard_map/cond/branch_1_fun/all_to_all | solution.py:231
  105.1 1.5 %backward.4 = f32[16,20,4,128]{3,2,1,0:T(4,128)} custom-call(s32[281]{0:T(512)S(1)} %get-tuple-element.50.plan_ref, f32[8,4,16,4,128]{4,3,2,1,0:T(4,128)S(1)} %bitcast.23, f32[2,128,512]{2,1,0:T(8,128)S(1)} %get-tuple-element.58.after_ref.refs_0_), custom_call_target="tpu_custom_call" | custom-call | bytes 1000000 | tf_op jit(solution)/shard_map/cond/branch_1_fun/backward/pallas_call | solution.py:307
  106.6 8.9 %all-to-all-start.7 = ((f32[16,20,4,128]{3,2,1,0:T(4,128)}), f32[16,20,4,128]{3,2,1,0:T(4,128)S(1)}, u32[]{:S(2)}, u32[]{:S(2)}) async-start(f32[16,20,4,128]{3,2,1,0:T(4,128)} %backward.4), calls=%async_computation.7 | async-start | bytes 1310720 | tf_op jit(solution)/shard_map/cond/branch_1_fun/all_to_all | solution.py:231
  115.6 3.4 %collective-permute-start.10 = (f32[2,128,512]{2,1,0:T(8,128)}, f32[2,128,512]{2,1,0:T(8,128)S(1)}, u32[]{:S(2)}, u32[]{:S(2)}) collective-permute-start(f32[2,128,512]{2,1,0:T(8,128)} %get-tuple-element.62), channel_id=1, source_target_pairs={{0,2},{1,3},{2,0},{3,1},{4,6},{5,7},{6,4},{7,5},{8,10},{9,11},{10,... | collective-permute-start | bytes 1572872 | tf_op jit(solution)/shard_map/cond/branch_1_fun/ppermute | solution.py:238
  119.0 3.1 %collective-permute-start.11 = (f32[2,128,512]{2,1,0:T(8,128)}, f32[2,128,512]{2,1,0:T(8,128)S(1)}, u32[]{:S(2)}, u32[]{:S(2)}) collective-permute-start(f32[2,128,512]{2,1,0:T(8,128)} %get-tuple-element.63), channel_id=1, source_target_pairs={{0,3},{1,0},{2,1},{3,2},{4,7},{5,4},{6,5},{7,6},{8,11},{9,8},{10,9... | collective-permute-start | bytes 1572872 | tf_op jit(solution)/shard_map/cond/branch_1_fun/ppermute | solution.py:238
  122.1 2.8 %collective-permute-start.9 = (f32[2,128,512]{2,1,0:T(8,128)S(1)}, f32[2,128,512]{2,1,0:T(8,128)S(1)}, u32[]{:S(2)}, u32[]{:S(2)}) collective-permute-start(f32[2,128,512]{2,1,0:T(8,128)S(1)} %get-tuple-element.61), channel_id=1, source_target_pairs={{0,1},{1,2},{2,3},{3,0},{4,5},{5,6},{6,7},{7,4},{8,9},{9,10},{10,1... | collective-permute-start | bytes 1572872 | tf_op jit(solution)/shard_map/cond/branch_1_fun/ppermute | solution.py:238
  124.9 9.2 %collective-permute-done.10.refs_2_ = f32[2,128,512]{2,1,0:T(8,128)S(1)} collective-permute-done((f32[2,128,512]{2,1,0:T(8,128)}, f32[2,128,512]{2,1,0:T(8,128)S(1)}, u32[]{:S(2)}, u32[]{:S(2)}) %collective-permute-start.10) | collective-permute-done | bytes 524320 | tf_op jit(solution)/shard_map/cond/branch_1_fun/ppermute | solution.py:238
  134.1 8.0 %collective-permute-done.11.refs_3_ = f32[2,128,512]{2,1,0:T(8,128)S(1)} collective-permute-done((f32[2,128,512]{2,1,0:T(8,128)}, f32[2,128,512]{2,1,0:T(8,128)S(1)}, u32[]{:S(2)}, u32[]{:S(2)}) %collective-permute-start.11) | collective-permute-done | bytes 524320 | tf_op jit(solution)/shard_map/cond/branch_1_fun/ppermute | solution.py:238
  142.0 1.1 collective-permute-done.9.refs_1_
  143.1 5.8 %all-to-all-done.7.back_ref = f32[16,20,4,128]{3,2,1,0:T(4,128)S(1)} async-done(((f32[16,20,4,128]{3,2,1,0:T(4,128)}), f32[16,20,4,128]{3,2,1,0:T(4,128)S(1)}, u32[]{:S(2)}, u32[]{:S(2)}) %all-to-all-start.7) | async-done | bytes 655392 | tf_op jit(solution)/shard_map/cond/branch_1_fun/all_to_all | solution.py:231
  149.0 3.0 %finish.4 = (f32[216,4,128]{2,1,0:T(4,128)}, f32[3,128,512]{2,1,0:T(8,128)}, f32[3,128,512]{2,1,0:T(8,128)}) custom-call(s32[281]{0:T(512)S(1)} %get-tuple-element.50.plan_ref, f32[16,20,4,128]{3,2,1,0:T(4,128)S(1)} %all-to-all-done.7.back_ref, f32[3,128,512]{2,1,0:T(8,128)} %get-tuple-element.59.left_hbm, f32[3,128,512]{2,1,0:T(8,128)} %get-tuple-element.60.right_hbm, ...), custom_call_target="tpu_custom_call" | custom-call | bytes 6000000 | tf_op jit(solution)/shard_map/cond/branch_1_fun/finish/pallas_call | solution.py:317
Async XLA Ops:
  0.6 5.7 %copy-start.12 = (bf16[3,128,512]{2,1,0:T(8,128)(2,1)S(1)}, bf16[3,128,512]{2,1,0:T(8,128)(2,1)}, u32[]{:S(2)}) copy-start(bf16[3,128,512]{2,1,0:T(8,128)(2,1)} %param.17) | copy-start | bytes 1179652
  6.4 15.4 %copy-start.14 = (bf16[3,512,128]{2,1,0:T(8,128)(2,1)S(1)}, bf16[3,512,128]{2,1,0:T(8,128)(2,1)}, u32[]{:S(2)}) copy-start(bf16[3,512,128]{2,1,0:T(8,128)(2,1)} %get-tuple-element.53.right_ref) | copy-start | bytes 1179652 | tf_op jit(solution)/shard_map/cond
  6.4 49.2 %all-to-all-start.4 = ((f32[16,20,4,128]{3,2,1,0:T(4,128)}), f32[16,20,4,128]{3,2,1,0:T(4,128)S(1)}, u32[]{:S(2)}, u32[]{:S(2)}) async-start(f32[16,20,4,128]{3,2,1,0:T(4,128)} %get-tuple-element.51), calls=%async_computation.4 | async-start | bytes 1310720 | tf_op jit(solution)/shard_map/cond/branch_1_fun/all_to_all | solution.py:231
  22.5 16.9 %collective-permute-start.6 = (f32[8,128,128]{2,1,0:T(8,128)S(1)}, f32[8,128,128]{2,1,0:T(8,128)S(1)}, u32[]{:S(2)}, u32[]{:S(2)}) collective-permute-start(f32[8,128,128]{2,1,0:T(8,128)S(1)} %get-tuple-element.55), channel_id=1, source_target_pairs={{0,1},{1,2},{2,3},{3,0},{4,5},{5,6},{6,7},{7,4},{8,9},{9,10},{10,1... | collective-permute-start | bytes 1572872 | tf_op jit(solution)/shard_map/cond/branch_1_fun/ppermute | solution.py:238
  26.0 25.2 %collective-permute-start.7 = (f32[8,128,128]{2,1,0:T(8,128)S(1)}, f32[8,128,128]{2,1,0:T(8,128)S(1)}, u32[]{:S(2)}, u32[]{:S(2)}) collective-permute-start(f32[8,128,128]{2,1,0:T(8,128)S(1)} %get-tuple-element.56), channel_id=1, source_target_pairs={{0,2},{1,3},{2,0},{3,1},{4,6},{5,7},{6,4},{7,5},{8,10},{9,11},{10,... | collective-permute-start | bytes 1572872 | tf_op jit(solution)/shard_map/cond/branch_1_fun/ppermute | solution.py:238
  30.8 21.7 %collective-permute-start.8 = (f32[8,128,128]{2,1,0:T(8,128)S(1)}, f32[8,128,128]{2,1,0:T(8,128)S(1)}, u32[]{:S(2)}, u32[]{:S(2)}) collective-permute-start(f32[8,128,128]{2,1,0:T(8,128)S(1)} %get-tuple-element.57), channel_id=1, source_target_pairs={{0,3},{1,0},{2,1},{3,2},{4,7},{5,4},{6,5},{7,6},{8,11},{9,8},{10,9... | collective-permute-start | bytes 1572872 | tf_op jit(solution)/shard_map/cond/branch_1_fun/ppermute | solution.py:238
  51.2 5.2 %copy-start.2 = (f32[8,128,128]{2,1,0:T(8,128)}, f32[8,128,128]{2,1,0:T(8,128)S(1)}, u32[]{:S(2)}) copy-start(f32[8,128,128]{2,1,0:T(8,128)S(1)} %collective-permute-done.7.refs_2_) | copy-start | bytes 1572868 | tf_op jit(solution)/shard_map/cond
  52.5 3.8 %copy-start.8 = (f32[8,128,128]{2,1,0:T(8,128)}, f32[8,128,128]{2,1,0:T(8,128)S(1)}, u32[]{:S(2)}) copy-start(f32[8,128,128]{2,1,0:T(8,128)S(1)} %collective-permute-done.8.refs_3_) | copy-start | bytes 1572868 | tf_op jit(solution)/shard_map/cond
  56.4 24.4 %copy-start.3 = (f32[8,128,128]{2,1,0:T(8,128)S(1)}, f32[8,128,128]{2,1,0:T(8,128)}, u32[]{:S(2)}) copy-start(f32[8,128,128]{2,1,0:T(8,128)} %copy-done.2) | copy-start | bytes 1572868 | tf_op jit(solution)/shard_map/cond
  56.4 24.4 %copy-start.9 = (f32[8,128,128]{2,1,0:T(8,128)S(1)}, f32[8,128,128]{2,1,0:T(8,128)}, u32[]{:S(2)}) copy-start(f32[8,128,128]{2,1,0:T(8,128)} %copy-done.8) | copy-start | bytes 1572868 | tf_op jit(solution)/shard_map/cond
  84.1 21.0 %all-to-all-start.6 = ((f32[32,16,4,128]{3,2,1,0:T(4,128)}), f32[32,16,4,128]{3,2,1,0:T(4,128)S(1)}, u32[]{:S(2)}, u32[]{:S(2)}) async-start(f32[32,16,4,128]{3,2,1,0:T(4,128)} %bitcast.6), calls=%async_computation.6 | async-start | bytes 2097152 | tf_op jit(solution)/shard_map/cond/branch_1_fun/all_to_all | solution.py:231
  106.6 42.3 %all-to-all-start.7 = ((f32[16,20,4,128]{3,2,1,0:T(4,128)}), f32[16,20,4,128]{3,2,1,0:T(4,128)S(1)}, u32[]{:S(2)}, u32[]{:S(2)}) async-start(f32[16,20,4,128]{3,2,1,0:T(4,128)} %backward.4), calls=%async_computation.7 | async-start | bytes 1310720 | tf_op jit(solution)/shard_map/cond/branch_1_fun/all_to_all | solution.py:231
  115.6 18.5 %collective-permute-start.10 = (f32[2,128,512]{2,1,0:T(8,128)}, f32[2,128,512]{2,1,0:T(8,128)S(1)}, u32[]{:S(2)}, u32[]{:S(2)}) collective-permute-start(f32[2,128,512]{2,1,0:T(8,128)} %get-tuple-element.62), channel_id=1, source_target_pairs={{0,2},{1,3},{2,0},{3,1},{4,6},{5,7},{6,4},{7,5},{8,10},{9,11},{10,... | collective-permute-start | bytes 1572872 | tf_op jit(solution)/shard_map/cond/branch_1_fun/ppermute | solution.py:238
  119.0 23.0 %collective-permute-start.11 = (f32[2,128,512]{2,1,0:T(8,128)}, f32[2,128,512]{2,1,0:T(8,128)S(1)}, u32[]{:S(2)}, u32[]{:S(2)}) collective-permute-start(f32[2,128,512]{2,1,0:T(8,128)} %get-tuple-element.63), channel_id=1, source_target_pairs={{0,3},{1,0},{2,1},{3,2},{4,7},{5,4},{6,5},{7,6},{8,11},{9,8},{10,9... | collective-permute-start | bytes 1572872 | tf_op jit(solution)/shard_map/cond/branch_1_fun/ppermute | solution.py:238
  122.1 21.0 %collective-permute-start.9 = (f32[2,128,512]{2,1,0:T(8,128)S(1)}, f32[2,128,512]{2,1,0:T(8,128)S(1)}, u32[]{:S(2)}, u32[]{:S(2)}) collective-permute-start(f32[2,128,512]{2,1,0:T(8,128)S(1)} %get-tuple-element.61), channel_id=1, source_target_pairs={{0,1},{1,2},{2,3},{3,0},{4,5},{5,6},{6,7},{7,4},{8,9},{9,10},{10,1... | collective-permute-start | bytes 1572872 | tf_op jit(solution)/shard_map/cond/branch_1_fun/ppermute | solution.py:238
